TPU v7x, 32 devices: a whole 2x2x4 slice. The times are simulated.
32 devices in a mesh: ens: 4 (over y, x), grid: 8 (over z, core).
Axes of the slice: x: 2, y: 2, z: 4, core: 2. Of those that a mesh axis runs over, the one named last changes fastest.
Arguments:
- grid_latent: bfloat16 [4, 8192, 512], P('ens', 'grid'), may hold values from -6 to 6
- mesh_latent: bfloat16 [4, 1024, 512], P('ens', 'grid'), may hold values from -6 to 6
- cotangent: bfloat16 [4, 1024, 512], P('ens', 'grid'), may hold values from -6 to 6
- edge_weights: bfloat16 [64, 2, 128, 128], P('grid'), may hold values from -0.125 to 0.125
- edge_targets: int32 [64, 2], P('grid'), may hold values from 0 to 7, as said below
- mesh_weights: bfloat16 [8, 2, 128, 128], P('grid'), may hold values from -0.375 to 0.375
- mesh_sources: int32 [8, 2], P('grid'), may hold values from 0 to 7, as said below
- encode_weight: bfloat16 [512, 512], replicated, may hold values from -0.25 to 0.25
- aggregate_weight: bfloat16 [512, 512], replicated, may hold values from -0.25 to 0.25
- process_weight: bfloat16 [512, 512], replicated, may hold values from -0.25 to 0.25
Outputs:
- result: bfloat16 [4, 1024, 512], P('ens', 'grid')
- grid_grad: bfloat16 [4, 8192, 512], P('ens', 'grid')
- grad_encode: float32 [512, 512], P('grid')
Inputs may be any that keep to these rules, and one draw needn't show every extreme that they name: `edge_targets`: row b names 2 different mesh blocks, each at most one away from b // 8. `mesh_sources`: row t names 2 different mesh blocks, each at most one away from t.
All inputs are finite; a program needn't handle non-finite values.
Results may differ from a plain program's by a relative error of at most 0.018.
Values may be sent and summed in bfloat16 or wider, within the bound.
A program may use at most 64 MiB of HBM per device.

v0:
```python
import jax
import jax.numpy as jnp
from jax import lax
from jax.sharding import PartitionSpec as P


def passed_along(value, axis, steps):
    count = lax.axis_size(axis)
    initial, last = (max(0, -steps), min(count, count - steps))
    return lax.ppermute(value, axis, [(source, source + steps) for source in range(initial, last)])


def with_halo(cells, sides, width):
    for axis, dim in sides:
        count = lax.axis_size(axis)
        ends = count - 1
        head = lax.slice_in_dim(cells, 0, width, axis=dim)
        tail = lax.slice_in_dim(cells, cells.shape[dim] - width, cells.shape[dim], axis=dim)
        cells = jnp.concatenate(
            [
                lax.ppermute(tail, axis, [(i, (i + 1) % count) for i in range(ends)]),
                cells,
                lax.ppermute(head, axis, [((i + 1) % count, i) for i in range(ends)]),
            ],
            axis=dim,
        )
    return cells


def silu_slope(value):
    sig = jax.nn.sigmoid(value)
    return sig * (1.0 + value * (1.0 - sig))


def on_device(
    grid_latent,
    mesh_latent,
    cotangent,
    edge_weights,
    edge_targets,
    mesh_weights,
    mesh_sources,
    encode_weight,
    aggregate_weight,
    process_weight,
):
    here = lax.axis_index("grid")
    blocks, slots, rows, unused = edge_weights.shape
    width = grid_latent.shape[2]
    three = jnp.arange(3, dtype=jnp.int32)
    target_pick = ((edge_targets - here + 1)[:, :, None] == three).astype(jnp.bfloat16)
    source_pick = ((mesh_sources[0] - here + 1)[:, None] == three).astype(jnp.bfloat16)
    grid_x = grid_latent[0]
    encoded = jnp.dot(grid_x, encode_weight, preferred_element_type=jnp.float32)
    messages = jax.nn.silu(encoded).astype(jnp.bfloat16).reshape(blocks, rows, width)
    products = jnp.einsum(
        "bkac,bcd->bkad", edge_weights, messages, preferred_element_type=jnp.float32
    )
    panels = jnp.einsum("bkj,bkad->jad", target_pick.astype(jnp.float32), products).astype(
        jnp.bfloat16
    )
    arrived = panels[1].astype(jnp.float32)
    for offset in (1, -1):
        arrived = arrived + passed_along(panels[offset + 1], "grid", offset).astype(jnp.float32)
    aggregated = arrived.astype(jnp.bfloat16)
    mesh_pre = jnp.dot(aggregated, aggregate_weight, preferred_element_type=jnp.float32)
    updated = (mesh_latent[0].astype(jnp.float32) + jax.nn.silu(mesh_pre)).astype(jnp.bfloat16)
    widened = with_halo(updated[None], (("grid", 1),), rows)
    nearby = widened[0].reshape(3, rows, width)
    chosen = jnp.einsum(
        "kj,jbd->kbd", source_pick, nearby, preferred_element_type=jnp.float32
    ).astype(jnp.bfloat16)
    processed = jnp.einsum(
        "kab,kbd->ad", mesh_weights[0], chosen, preferred_element_type=jnp.float32
    ).astype(jnp.bfloat16)
    proc_pre = jnp.dot(processed, process_weight, preferred_element_type=jnp.float32)
    result = (updated.astype(jnp.float32) + jax.nn.silu(proc_pre)).astype(jnp.bfloat16)
    upstream = cotangent[0].astype(jnp.float32)
    proc_delta = (upstream * silu_slope(proc_pre)).astype(jnp.bfloat16)
    proc_back = jnp.einsum(
        "ae,de->ad", proc_delta, process_weight, preferred_element_type=jnp.float32
    ).astype(jnp.bfloat16)
    back = jnp.einsum("kab,ad->kbd", mesh_weights[0], proc_back, preferred_element_type=jnp.float32)
    pushed = jnp.einsum("kj,kbd->jbd", source_pick.astype(jnp.float32), back).astype(jnp.bfloat16)
    mesh_grad = upstream + pushed[1].astype(jnp.float32)
    for offset in (1, -1):
        mesh_grad = mesh_grad + passed_along(pushed[offset + 1], "grid", offset).astype(jnp.float32)
    mesh_delta = (mesh_grad * silu_slope(mesh_pre)).astype(jnp.bfloat16)
    agg_grad = jnp.einsum(
        "ae,de->ad", mesh_delta, aggregate_weight, preferred_element_type=jnp.float32
    ).astype(jnp.bfloat16)
    returned = with_halo(agg_grad[None], (("grid", 1),), rows)
    returned = returned[0].reshape(3, rows, width)
    picked = jnp.einsum(
        "bkj,jad->bkad", target_pick, returned, preferred_element_type=jnp.float32
    ).astype(jnp.bfloat16)
    message_grad = jnp.einsum(
        "bkac,bkad->bcd", edge_weights, picked, preferred_element_type=jnp.float32
    )
    message_grad = message_grad.reshape(blocks * rows, width)
    enc_delta = (message_grad * silu_slope(encoded)).astype(jnp.bfloat16)
    grad_enc = jnp.einsum("rd,re->de", grid_x, enc_delta, preferred_element_type=jnp.float32)
    grid_grad = jnp.einsum(
        "re,de->rd", enc_delta, encode_weight, preferred_element_type=jnp.float32
    ).astype(jnp.bfloat16)
    members = lax.axis_size("ens")
    bands = lax.axis_size("grid")
    grid_scale = 1.0 / float(members * blocks * rows * bands) ** 0.5
    partial_grad = grad_enc * grid_scale
    summed = lax.psum(partial_grad, ("ens", "grid"))
    share = width // bands
    final = lax.dynamic_slice_in_dim(summed, here * share, share, 0)
    return (result[None], grid_grad[None], final)


def solution(mesh):
    return jax.shard_map(
        on_device,
        mesh=mesh,
        in_specs=(
            P("ens", "grid", None),
            P("ens", "grid", None),
            P("ens", "grid", None),
            P("grid", None, None, None),
            P("grid", None),
            P("grid", None, None, None),
            P("grid", None),
            P(),
            P(),
            P(),
        ),
        out_specs=(P("ens", "grid", None), P("ens", "grid", None), P("grid", None)),
        check_vma=False,
    )
```

profile of v0, /device:TPU:0, one launch (start us, length us, event | category | flops | bytes accessed | tf_op | source)
XLA Modules:
  0.0 203.0 jit_solution(11321193817579130908)
XLA Ops:
  7.2 0.0 copy-start
  7.2 0.0 all-reduce.2.cloned.1.call-start
  7.2 1.2 copy-done
  8.4 0.0 copy-start.1
  8.4 3.3 %multiply_convert_fusion = (bf16[1024,512]{1,0:T(8,128)(2,1)S(1)}, f32[1024,512]{1,0:T(8,128)}) fusion(bf16[512,512]{1,0:T(8,128)(2,1)} %param.17, bf16[1,1024,512]{2,1,0:T(8,128)(2,1)S(1)} %copy-done), kind=kOutput, calls=%fused_computation.5 | convolution fusion | flops 539492352 | bytes 4718592 | tf_op jit(solution)/shard_map/dot_general | solution.py:54
  11.7 0.0 copy-done.1
  11.7 0.8 convolution_bitcast_fusion
  12.5 0.0 copy-start.6
  12.5 2.9 %copy.23 = bf16[8,2,128,512]{3,0,1,2:T(8,128)(2,1)} copy(bf16[8,2,128,512]{2,3,1,0:T(8,128)(2,1)S(1)} %convolution_bitcast_fusion) | data formatting | bytes 4194304 | tf_op jit(solution)/shard_map/bkac,bcd->bkad/dot_general | solution.py:56
  15.5 0.0 copy-done.6
  15.5 0.0 copy-start.7
  15.5 0.0 copy-start.9
  15.5 2.2 %fusion.5 = bf16[3,128,512]{2,0,1:T(4,128)(2,1)S(1)} fusion(bf16[8,2,128,512]{3,0,1,2:T(8,128)(2,1)} %copy.23, s32[8,2]{0,1:T(2,128)S(1)} %subtract_add_fusion), kind=kOutput, calls=%fused_computation.13 | convolution fusion | flops 6291504 | bytes 2490432 | tf_op jit(solution)/shard_map/bkj,bkad->jad/dot_general | solution.py:59
  17.7 0.0 copy-start.11
  17.7 0.5 fusion.55
  18.3 1.3 collective-permute-start.1
  19.6 0.0 copy-start.4
  19.6 0.0 copy-start.5
  19.6 3.2 %collective-permute-start = (bf16[128,512]{1,0:T(8,128)(2,1)S(1)}, bf16[128,512]{1,0:T(8,128)(2,1)S(1)}, u32[]{:S(2)}, u32[]{:S(2)}) collective-permute-start(bf16[128,512]{1,0:T(8,128)(2,1)S(1)} %bitcast.133), channel_id=1, source_target_pairs={{0,1},{1,2},{2,3},{3,4},{4,5},{5,6},{6,7},{8,9},{9,10},{10,11},{11... | collective-permute-start | bytes 393224 | tf_op jit(solution)/shard_map/ppermute | solution.py:10
  22.8 0.0 collective-permute-done.1
  22.8 1.0 collective-permute-done
  23.8 0.0 copy-done.7
  23.8 0.0 copy-done.9
  23.8 0.0 copy-start.10
  23.8 0.3 fusion.23
  24.1 1.3 collective-permute-start.3
  25.4 6.1 %collective-permute-start.2 = (bf16[1,128,512]{2,1,0:T(8,128)(2,1)S(1)}, bf16[1,128,512]{2,1,0:T(8,128)(2,1)S(1)}, u32[]{:S(2)}, u32[]{:S(2)}) collective-permute-start(bf16[1,128,512]{2,1,0:T(8,128)(2,1)S(1)} %bitcast.129), channel_id=1, source_target_pairs={{0,1},{1,2},{2,3},{3,4},{4,5},{5,6},{6,7},{8,9},{9,10},{10,11},{11... | collective-permute-start | bytes 393224 | tf_op jit(solution)/shard_map/ppermute | solution.py:21
  31.5 0.0 copy-done.11
  31.5 0.0 collective-permute-done.3
  31.5 0.9 collective-permute-done.2
  32.5 0.5 convolution_convert_fusion.2
  33.0 0.0 copy-done.4
  33.0 0.0 copy-done.5
  33.0 0.5 fusion.9
  33.6 0.0 copy-done.10
  33.6 0.6 convolution_bitcast_fusion.2
  34.2 0.2 copy.27
  34.4 0.6 fusion.47
  35.0 0.1 copy.61
  35.1 5.3 %collective-permute-start.4 = (bf16[128,512]{1,0:T(8,128)(2,1)S(1)}, bf16[128,512]{1,0:T(8,128)(2,1)S(1)}, u32[]{:S(2)}, u32[]{:S(2)}) collective-permute-start(bf16[128,512]{1,0:T(8,128)(2,1)S(1)} %get-tuple-element.15), channel_id=1, source_target_pairs={{0,1},{1,2},{2,3},{3,4},{4,5},{5,6},{6,7},{8,9},{9,10},{10,11},{11... | collective-permute-start | bytes 393224 | tf_op jit(solution)/shard_map/ppermute | solution.py:10
  40.4 1.3 collective-permute-start.5
  41.7 0.0 collective-permute-done.4
  41.7 3.9 %collective-permute-done.5 = bf16[128,512]{1,0:T(8,128)(2,1)S(1)} collective-permute-done((bf16[128,512]{1,0:T(8,128)(2,1)S(1)}, bf16[128,512]{1,0:T(8,128)(2,1)S(1)}, u32[]{:S(2)}, u32[]{:S(2)}) %collective-permute-start.5) | collective-permute-done | bytes 131104 | tf_op jit(solution)/shard_map/ppermute | solution.py:10
  45.6 0.3 fusion.8
  45.9 0.0 copy-start.2
  45.9 1.4 collective-permute-start.7
  47.4 6.1 %collective-permute-start.6 = (bf16[1,128,512]{2,1,0:T(8,128)(2,1)S(1)}, bf16[1,128,512]{2,1,0:T(8,128)(2,1)S(1)}, u32[]{:S(2)}, u32[]{:S(2)}) collective-permute-start(bf16[1,128,512]{2,1,0:T(8,128)(2,1)S(1)} %fusion.8), channel_id=1, source_target_pairs={{0,1},{1,2},{2,3},{3,4},{4,5},{5,6},{6,7},{8,9},{9,10},{10,11},{11... | collective-permute-start | bytes 393224 | tf_op jit(solution)/shard_map/ppermute | solution.py:21
  53.5 0.0 collective-permute-done.7
  53.5 1.0 collective-permute-done.6
  54.4 1.0 convolution_convert_fusion
  55.5 0.0 copy-done.2
  55.5 0.0 copy-start.3
  55.5 1.4 fusion.1
  56.9 0.2 copy-done.3
  57.1 0.8 fusion
  57.8 0.0 copy-start.8
  57.8 1.7 fusion.3
  59.5 0.0 all-reduce.2.cloned.1.call-update
  59.6 0.7 fusion.37
  60.3 0.0 copy-done.8
  60.3 1.7 fusion.4
  62.0 132.2 %all-reduce.2.cloned.1.call-done = f32[512,512]{0,1:T(8,128)} async-done(((f32[512,512]{0,1:T(8,128)}), f32[512,512]{0,1:T(8,128)}) %all-reduce.2.cloned.1.call-update) | async-done | bytes 1048592 | tf_op jit(solution)/shard_map/psum | solution.py:110
  194.2 1.1 constant_dynamic-slice_fusion
  195.3 0.8 copy.32
  (7 shorter events, 0.1 us)
Async XLA Ops:
  7.2 1.2 copy-start
  7.2 187.1 %all-reduce.2.cloned.1.call-start = ((), (), s32[]{:S(2)}) async-start(), calls=%async_computation | async-start | bytes 2097152 | tf_op jit(solution)/shard_map/psum | solution.py:110
  8.4 3.4 %copy-start.1 = (bf16[8,2,128,128]{3,2,1,0:T(8,128)(2,1)S(1)}, bf16[8,2,128,128]{3,2,1,0:T(8,128)(2,1)}, u32[]{:S(2)}) copy-start(bf16[8,2,128,128]{3,2,1,0:T(8,128)(2,1)} %param.13) | copy-start | bytes 1572868
  12.5 3.0 %copy-start.6 = (s32[8,2]{0,1:T(2,128)S(1)}, s32[8,2]{0,1:T(2,128)}, u32[]{:S(2)}) copy-start(s32[8,2]{0,1:T(2,128)} %param.14) | copy-start | bytes 196
  15.5 8.3 %copy-start.7 = (bf16[512,512]{1,0:T(8,128)(2,1)S(1)}, bf16[512,512]{1,0:T(8,128)(2,1)}, u32[]{:S(2)}) copy-start(bf16[512,512]{1,0:T(8,128)(2,1)} %param.18) | copy-start | bytes 1572868
  15.5 8.3 %copy-start.9 = (bf16[1,128,512]{2,1,0:T(8,128)(2,1)S(1)}, bf16[1,128,512]{2,1,0:T(8,128)(2,1)}, u32[]{:S(2)}) copy-start(bf16[1,128,512]{2,1,0:T(8,128)(2,1)} %param.11) | copy-start | bytes 393220
  17.7 13.8 %copy-start.11 = (s32[1,2]{1,0:T(1,128)S(1)}, s32[1,2]{1,0:T(1,128)}, u32[]{:S(2)}) copy-start(s32[1,2]{1,0:T(1,128)} %param.16) | copy-start | bytes 28
  18.3 4.5 %collective-permute-start.1 = (bf16[128,512]{1,0:T(8,128)(2,1)S(1)}, bf16[128,512]{1,0:T(8,128)(2,1)S(1)}, u32[]{:S(2)}, u32[]{:S(2)}) collective-permute-start(bf16[128,512]{1,0:T(8,128)(2,1)S(1)} %bitcast.132), channel_id=1, source_target_pairs={{1,0},{2,1},{3,2},{4,3},{5,4},{6,5},{7,6},{9,8},{10,9},{11,10},{12... | collective-permute-start | bytes 393224 | tf_op jit(solution)/shard_map/ppermute | solution.py:10
  19.6 13.4 %copy-start.4 = (bf16[512,512]{1,0:T(8,128)(2,1)S(1)}, bf16[512,512]{1,0:T(8,128)(2,1)}, u32[]{:S(2)}) copy-start(bf16[512,512]{1,0:T(8,128)(2,1)} %param.19) | copy-start | bytes 1572868
  19.6 13.4 %copy-start.5 = (bf16[1,2,128,128]{3,2,1,0:T(8,128)(2,1)S(1)}, bf16[1,2,128,128]{3,2,1,0:T(8,128)(2,1)}, u32[]{:S(2)}) copy-start(bf16[1,2,128,128]{3,2,1,0:T(8,128)(2,1)} %param.15) | copy-start | bytes 196612
  19.6 4.1 %collective-permute-start = (bf16[128,512]{1,0:T(8,128)(2,1)S(1)}, bf16[128,512]{1,0:T(8,128)(2,1)S(1)}, u32[]{:S(2)}, u32[]{:S(2)}) collective-permute-start(bf16[128,512]{1,0:T(8,128)(2,1)S(1)} %bitcast.133), channel_id=1, source_target_pairs={{0,1},{1,2},{2,3},{3,4},{4,5},{5,6},{6,7},{8,9},{9,10},{10,11},{11... | collective-permute-start | bytes 393224 | tf_op jit(solution)/shard_map/ppermute | solution.py:10
  23.8 9.8 %copy-start.10 = (bf16[1,128,512]{2,1,0:T(8,128)(2,1)S(1)}, bf16[1,128,512]{2,1,0:T(8,128)(2,1)}, u32[]{:S(2)}) copy-start(bf16[1,128,512]{2,1,0:T(8,128)(2,1)} %param.12) | copy-start | bytes 393220
  24.1 7.5 %collective-permute-start.3 = (bf16[1,128,512]{2,1,0:T(8,128)(2,1)S(1)}, bf16[1,128,512]{2,1,0:T(8,128)(2,1)S(1)}, u32[]{:S(2)}, u32[]{:S(2)}) collective-permute-start(bf16[1,128,512]{2,1,0:T(8,128)(2,1)S(1)} %bitcast.128), channel_id=1, source_target_pairs={{1,0},{2,1},{3,2},{4,3},{5,4},{6,5},{7,6},{9,8},{10,9},{11,10},{12... | collective-permute-start | bytes 393224 | tf_op jit(solution)/shard_map/ppermute | solution.py:23
  25.4 7.1 %collective-permute-start.2 = (bf16[1,128,512]{2,1,0:T(8,128)(2,1)S(1)}, bf16[1,128,512]{2,1,0:T(8,128)(2,1)S(1)}, u32[]{:S(2)}, u32[]{:S(2)}) collective-permute-start(bf16[1,128,512]{2,1,0:T(8,128)(2,1)S(1)} %bitcast.129), channel_id=1, source_target_pairs={{0,1},{1,2},{2,3},{3,4},{4,5},{5,6},{6,7},{8,9},{9,10},{10,11},{11... | collective-permute-start | bytes 393224 | tf_op jit(solution)/shard_map/ppermute | solution.py:21
  35.1 6.6 %collective-permute-start.4 = (bf16[128,512]{1,0:T(8,128)(2,1)S(1)}, bf16[128,512]{1,0:T(8,128)(2,1)S(1)}, u32[]{:S(2)}, u32[]{:S(2)}) collective-permute-start(bf16[128,512]{1,0:T(8,128)(2,1)S(1)} %get-tuple-element.15), channel_id=1, source_target_pairs={{0,1},{1,2},{2,3},{3,4},{4,5},{5,6},{6,7},{8,9},{9,10},{10,11},{11... | collective-permute-start | bytes 393224 | tf_op jit(solution)/shard_map/ppermute | solution.py:10
  40.4 5.2 %collective-permute-start.5 = (bf16[128,512]{1,0:T(8,128)(2,1)S(1)}, bf16[128,512]{1,0:T(8,128)(2,1)S(1)}, u32[]{:S(2)}, u32[]{:S(2)}) collective-permute-start(bf16[128,512]{1,0:T(8,128)(2,1)S(1)} %get-tuple-element.16), channel_id=1, source_target_pairs={{1,0},{2,1},{3,2},{4,3},{5,4},{6,5},{7,6},{9,8},{10,9},{11,10},{12... | collective-permute-start | bytes 393224 | tf_op jit(solution)/shard_map/ppermute | solution.py:10
  45.9 9.6 %copy-start.2 = (bf16[8,2,128,128]{3,2,1,0:T(8,128)(2,1)S(1)}, bf16[8,2,128,128]{3,2,1,0:T(8,128)(2,1)}, u32[]{:S(2)}) copy-start(bf16[8,2,128,128]{3,2,1,0:T(8,128)(2,1)} %param.13) | copy-start | bytes 1572868
  45.9 7.5 %collective-permute-start.7 = (bf16[1,128,512]{2,1,0:T(8,128)(2,1)S(1)}, bf16[1,128,512]{2,1,0:T(8,128)(2,1)S(1)}, u32[]{:S(2)}, u32[]{:S(2)}) collective-permute-start(bf16[1,128,512]{2,1,0:T(8,128)(2,1)S(1)} %fusion.8), channel_id=1, source_target_pairs={{1,0},{2,1},{3,2},{4,3},{5,4},{6,5},{7,6},{9,8},{10,9},{11,10},{12... | collective-permute-start | bytes 393224 | tf_op jit(solution)/shard_map/ppermute | solution.py:23
  47.4 7.1 %collective-permute-start.6 = (bf16[1,128,512]{2,1,0:T(8,128)(2,1)S(1)}, bf16[1,128,512]{2,1,0:T(8,128)(2,1)S(1)}, u32[]{:S(2)}, u32[]{:S(2)}) collective-permute-start(bf16[1,128,512]{2,1,0:T(8,128)(2,1)S(1)} %fusion.8), channel_id=1, source_target_pairs={{0,1},{1,2},{2,3},{3,4},{4,5},{5,6},{6,7},{8,9},{9,10},{10,11},{11... | collective-permute-start | bytes 393224 | tf_op jit(solution)/shard_map/ppermute | solution.py:21
  55.5 1.6 copy-start.3
  57.8 2.5 %copy-start.8 = (bf16[512,512]{1,0:T(8,128)(2,1)S(1)}, bf16[512,512]{1,0:T(8,128)(2,1)}, u32[]{:S(2)}) copy-start(bf16[512,512]{1,0:T(8,128)(2,1)} %param.17) | copy-start | bytes 1572868
Sparse Core Ops, SparseCore 0:
  59.7 134.5 all-reduce.1
where the time goes:
time: 203 us
  waiting for transfers between devices  139 us (68%)
  starting transfers between devices  26.1 us (13%)
  matrix products  14.9 us (7%)
  between operations  14.4 us (7%)
  local copies, waits for them, and re-layouts  6.56 us (3%)
  other arithmetic  2.1 us (1%)
    psum x1, waiting for transfers between devices, on_device(): summed = lax.psum(partial_grad, ('ens', 'grid'))  132 us
    ppermute x2, starting transfers between devices, with_halo(): lax.ppermute(tail, axis, [(i, (i + 1) % count) for i in range(ends)])  12.2 us
    ppermute x4, starting transfers between devices, passed_along(): lax.ppermute(value, axis, [(source, source + steps) for source in range(i...  11.1 us
    ppermute x4, waiting for transfers between devices, passed_along(): lax.ppermute(value, axis, [(source, source + steps) for source in range(i...  4.83 us
  transfers between devices with their start and end apart: 9, of which 5 were waited for; matrix products, arithmetic and copies ran while one was open for 1% of the time, Pallas kernels for 0%

commit v1 on v0

v1 whole, which is shorter than its diff:
```python
import functools

import jax
import jax.numpy as jnp
from jax import lax
from jax.experimental import pallas as pl
from jax.experimental.pallas import tpu as pltpu
from jax.sharding import PartitionSpec as P

MESH = pl.DeviceIdType.MESH
F32 = jnp.float32
BF16 = jnp.bfloat16
CHUNKS = 4


def sigmoid(value):
    return 0.5 + 0.5 * jnp.tanh(0.5 * value)


def slope_of(value):
    sig = sigmoid(value)
    return sig * (1.0 + value * (1.0 - sig))


def dot(a, b):
    return jnp.dot(a, b, preferred_element_type=F32)


def dot_t(a, b):
    return lax.dot_general(a, b, (((1,), (1,)), ((), ())), preferred_element_type=F32)


def kernel(
    bands, members, scale, fused,
    x_h, mesh_h, cot_h, edge_h, targets, mweight_h, sources, enc_w_h, agg_w_h, proc_w_h,
    result_h, grid_h, final_h,
    x, mesh, cot, edge, mweight, enc_w, agg_w, proc_w,
    wide, wide_own_t, wide_side_t, near, near_t, x_t,
    encoded, messages, panel_out, panel_in, upd, upd_in, push_out, push_in, agg, agg_in,
    own_grad, enc_delta, grid_out, result,
    part, part_out, pair_in, quarter, quarter_out, ens_in, summed, summed_out, z_in, final,
    in_sem, out_sem, halo_send, halo_recv, a_send, a_recv, b_send, b_recv, c_send, c_recv, d_send, d_recv,
):
    me = lax.axis_index("grid")
    ens = lax.axis_index("ens")
    core = lax.rem(me, 2)
    level = me // 2
    levels = bands // 2
    rows = mesh.shape[0]
    total = x.shape[0]
    blocks = total // rows
    step = total // CHUNKS
    width = x.shape[1]
    far = 2 * core - 1
    far_there = (me + far >= 0) & (me + far < bands)

    def both(act):
        pl.when(far_there)(lambda: act(far))
        act(-far)

    def local(src, dst, sem):
        copy = pltpu.make_async_copy(src, dst, sem)
        copy.start()
        return copy

    edge_copy = local(edge_h, edge, in_sem.at[0])
    enc_copy = local(enc_w_h, enc_w, in_sem.at[1])
    x_copies = [
        local(x_h.at[0, pl.ds(i * step, step)], x.at[pl.ds(i * step, step)], in_sem.at[8 + i])
        for i in range(CHUNKS)
    ]
    agg_copy = local(agg_w_h, agg_w, in_sem.at[2])
    mesh_copy = local(mesh_h.at[0], mesh, in_sem.at[3])
    mweight_copy = local(mweight_h.at[0], mweight, in_sem.at[4])
    proc_copy = local(proc_w_h, proc_w, in_sem.at[5])
    cot_copy = local(cot_h.at[0], cot, in_sem.at[6])

    barrier = pltpu.get_barrier_semaphore()

    def greet(**where):
        pl.semaphore_signal(barrier, inc=1, device_id=where, device_id_type=MESH)

    both(lambda off: greet(grid=me + off))
    expected = 1 + far_there.astype(jnp.int32)
    if fused:
        for d in range(1, members):
            greet(ens=lax.rem(ens + d, members))
        for d in range(1, levels):
            greet(grid=lax.rem(level + d, levels) * 2 + core)
        expected = expected + (members - 1) + (levels - 1)

    @pl.when(jnp.logical_not(far_there))
    def clear():
        slot = (1 + far) // 2
        for ref in (panel_in, upd_in, push_in, agg_in):
            ref[slot] = jnp.zeros(ref.shape[1:], ref.dtype)

    edge_copy.wait()
    for b in range(blocks):
        first = edge[b, 0].astype(F32)
        second = edge[b, 1].astype(F32)
        for j in range(3):
            hit = [jnp.where(targets[b, k] - me + 1 == j, 1.0, 0.0).astype(F32) for k in range(2)]
            wide[j, :, b * rows:(b + 1) * rows] = (first * hit[0] + second * hit[1]).astype(BF16)

    enc_copy.wait()
    for i in range(CHUNKS):
        x_copies[i].wait()
        span = pl.ds(i * step, step)
        value = dot(x[span], enc_w[...])
        encoded[span] = value
        messages[span] = (value * sigmoid(value)).astype(BF16)

    def halo(turn, source, landing, off):
        slot = (1 - off) // 2
        return pltpu.make_async_remote_copy(
            src_ref=source,
            dst_ref=landing.at[slot],
            send_sem=halo_send.at[turn, slot],
            recv_sem=halo_recv.at[turn, slot],
            device_id={"grid": me + off},
            device_id_type=MESH,
        )

    def received(turn, landing):
        act = lambda off: halo(turn, landing.at[(1 - off) // 2], landing, off).wait_recv()
        act(far)
        pl.when(far_there)(lambda: act(-far))

    def sent(turn, landing):
        both(lambda off: halo(turn, landing.at[(1 - off) // 2], landing, off).wait_send())

    pl.semaphore_wait(barrier, expected)
    for off, there in ((far, far_there), (-far, None)):
        panel_out[(1 - off) // 2] = dot(wide[1 + off], messages[...]).astype(BF16)
        go = functools.partial(halo, 0, panel_out.at[(1 - off) // 2], panel_in, off)
        if there is None:
            go().start()
        else:
            pl.when(there)(lambda: go().start())

    own_panel = dot(wide[1], messages[...])
    for i in range(CHUNKS):
        span = pl.ds(i * step, step)
        encoded[span] = slope_of(encoded[span])
    for b in range(blocks):
        span = pl.ds(b * rows, rows)
        wide_own_t[span] = wide[1, :, b * rows:(b + 1) * rows].T
        wide_side_t[span, 0:rows] = wide[0, :, b * rows:(b + 1) * rows].T
        wide_side_t[span, rows:2 * rows] = wide[2, :, b * rows:(b + 1) * rows].T
    mweight_copy.wait()
    first = mweight[0].astype(F32)
    second = mweight[1].astype(F32)
    for j in range(3):
        hit = [jnp.where(sources[0, k] - me + 1 == j, 1.0, 0.0).astype(F32) for k in range(2)]
        mixed = (first * hit[0] + second * hit[1]).astype(BF16)
        near[j] = mixed
        near_t[j] = mixed.T
    mesh_copy.wait()
    agg_copy.wait()

    received(0, panel_in)
    aggregated = own_panel + panel_in[0].astype(F32) + panel_in[1].astype(F32)
    mesh_pre = dot(aggregated.astype(BF16), agg_w[...])
    mesh_sig = sigmoid(mesh_pre)
    updated = (mesh[...].astype(F32) + mesh_pre * mesh_sig).astype(BF16)
    upd[...] = updated
    both(lambda off: halo(1, upd, upd_in, off).start())

    processed = dot(near[1], updated)
    mesh_slope = mesh_sig * (1.0 + mesh_pre * (1.0 - mesh_sig))
    deep = width // CHUNKS
    for i in range(CHUNKS):
        x_t[i] = x[:, i * deep:(i + 1) * deep].T
    proc_copy.wait()
    cot_copy.wait()
    upstream = cot[...].astype(F32)

    received(1, upd_in)
    processed = processed + dot(near[0], upd_in[0]) + dot(near[2], upd_in[1])
    proc_pre = dot(processed.astype(BF16), proc_w[...])
    proc_sig = sigmoid(proc_pre)
    proc_slope = proc_sig * (1.0 + proc_pre * (1.0 - proc_sig))
    proc_back = dot_t((upstream * proc_slope).astype(BF16), proc_w[...]).astype(BF16)
    for off, there in ((far, far_there), (-far, None)):
        push_out[(1 - off) // 2] = dot(near_t[1 + off], proc_back).astype(BF16)
        go = functools.partial(halo, 2, push_out.at[(1 - off) // 2], push_in, off)
        if there is None:
            go().start()
        else:
            pl.when(there)(lambda: go().start())
    mesh_grad = upstream + dot(near_t[1], proc_back)
    result[...] = (upd[...].astype(F32) + proc_pre * proc_sig).astype(BF16)
    result_copy = local(result, result_h.at[0], out_sem.at[CHUNKS])

    received(2, push_in)
    mesh_grad = mesh_grad + push_in[0].astype(F32) + push_in[1].astype(F32)
    agg_grad = dot_t((mesh_grad * mesh_slope).astype(BF16), agg_w[...]).astype(BF16)
    agg[...] = agg_grad
    both(lambda off: halo(3, agg, agg_in, off).start())
    for i in range(CHUNKS):
        span = pl.ds(i * step, step)
        own_grad[span] = dot(wide_own_t[span], agg_grad)

    received(3, agg_in)
    sides = agg_in[...].reshape(2 * rows, width)
    for i in range(CHUNKS):
        span = pl.ds(i * step, step)
        grad = own_grad[span] + dot(wide_side_t[span], sides)
        enc_delta[span] = (grad * encoded[span]).astype(BF16)

    def grid_part(i):
        span = pl.ds(i * step, step)
        grid_out[span] = dot_t(enc_delta[span], enc_w[...]).astype(BF16)
        return local(grid_out.at[span], grid_h.at[0, span], out_sem.at[i])

    if not fused:
        for i in range(CHUNKS):
            part[i] = dot(x_t[i], enc_delta[...]) * scale
        final_copy = local(part, final_h, out_sem.at[CHUNKS + 1])
        grid_copies = [grid_part(i) for i in range(CHUNKS)]
    else:
        share = part.shape[2]
        mine = share // members

        def pair(z):
            return pltpu.make_async_remote_copy(
                src_ref=part_out.at[z, 1 - core], dst_ref=pair_in.at[z],
                send_sem=a_send.at[z], recv_sem=a_recv.at[z],
                device_id={"grid": me + 1 - 2 * core}, device_id_type=MESH)

        def across(z, d, arriving):
            peer = lax.rem(ens + d, members)
            slot = peer if arriving else ens
            return pltpu.make_async_remote_copy(
                src_ref=quarter_out.at[z, peer], dst_ref=ens_in.at[z, slot],
                send_sem=b_send.at[z, peer], recv_sem=b_recv.at[z, slot],
                device_id={"ens": peer}, device_id_type=MESH)

        def along(d, arriving):
            peer = lax.rem(level + d, levels)
            slot = peer if arriving else level
            return pltpu.make_async_remote_copy(
                src_ref=summed_out.at[peer], dst_ref=z_in.at[slot],
                send_sem=c_send.at[peer], recv_sem=c_recv.at[slot],
                device_id={"grid": peer * 2 + core}, device_id_type=MESH)

        def gather(d, arriving):
            peer = lax.rem(ens + d, members)
            slot = peer if arriving else ens
            return pltpu.make_async_remote_copy(
                src_ref=final.at[ens], dst_ref=final.at[slot],
                send_sem=d_send.at[peer], recv_sem=d_recv.at[slot],
                device_id={"ens": peer}, device_id_type=MESH)

        order = [lax.rem(level + d, levels) for d in list(range(1, levels)) + [0]]
        for z in order:
            value = (dot(x_t[z], enc_delta[...]) * scale).reshape(2, share, width)
            part[z] = value
            part_out[z] = value.astype(BF16)
            pair(z).start()
        grid_copies = [grid_part(0)]
        for z in order:
            pair(z).wait_recv()
            value = part[z, core] + pair_in[z].astype(F32)
            value = value.reshape(members, mine, width)
            quarter[z] = value
            quarter_out[z] = value.astype(BF16)
            for d in range(1, members):
                across(z, d, False).start()
        grid_copies += [grid_part(i) for i in range(1, CHUNKS)]
        for n, z in enumerate(order):
            value = quarter[z, ens]
            for d in range(1, members):
                across(z, d, True).wait_recv()
                value = value + ens_in[z, lax.rem(ens + d, members)].astype(F32)
            if n < levels - 1:
                summed_out[z] = value.astype(BF16)
                along(n + 1, False).start()
            else:
                summed[...] = value
        value = summed[...]
        for d in range(1, levels):
            along(d, True).wait_recv()
            value = value + z_in[lax.rem(level + d, levels)].astype(F32)
        final[ens] = value
        for d in range(1, members):
            gather(d, False).start()
        for d in range(1, members):
            gather(d, True).wait_recv()
        final_copy = local(final, final_h, out_sem.at[CHUNKS + 1])
        for z in order:
            pair(z).wait_send()
            for d in range(1, members):
                across(z, d, False).wait_send()
        for d in range(1, levels):
            along(d, False).wait_send()
        for d in range(1, members):
            gather(d, False).wait_send()

    for turn, landing in enumerate((panel_in, upd_in, push_in, agg_in)):
        sent(turn, landing)
    result_copy.wait()
    for copy in grid_copies:
        copy.wait()
    final_copy.wait()


def on_device(
    bands, members,
    grid_latent, mesh_latent, cotangent, edge_weights, edge_targets, mesh_weights, mesh_sources,
    encode_weight, aggregate_weight, process_weight,
):
    unused, total, width = grid_latent.shape
    rows = mesh_latent.shape[1]
    share = width // bands
    levels = max(bands // 2, 1)
    fused = bands % 2 == 0 and levels == CHUNKS and share % (16 * members) == 0
    scale = 1.0 / float(members * total * bands) ** 0.5
    mine = share // members if fused else 16
    gshape = (CHUNKS, 2, width // CHUNKS // 2, width) if fused else (CHUNKS, width // CHUNKS, width)
    last = (members, mine, width) if fused else gshape
    vm = pltpu.VMEM
    dma = pltpu.SemaphoreType.DMA
    panel = (2, rows, width)
    quarters = (CHUNKS, members, mine, width)
    scratch = [
        vm((total, width), BF16), vm((rows, width), BF16), vm((rows, width), BF16),
        vm(edge_weights.shape, BF16), vm(mesh_weights.shape[1:], BF16),
        vm((width, width), BF16), vm((width, width), BF16), vm((width, width), BF16),
        vm((3, rows, total), BF16), vm((total, rows), BF16), vm((total, 2 * rows), BF16),
        vm((3, rows, rows), BF16), vm((3, rows, rows), BF16), vm((CHUNKS, width // CHUNKS, total), BF16),
        vm((total, width), F32), vm((total, width), BF16),
        vm(panel, BF16), vm(panel, BF16), vm((rows, width), BF16), vm(panel, BF16),
        vm(panel, BF16), vm(panel, BF16), vm((rows, width), BF16), vm(panel, BF16),
        vm((total, width), F32), vm((total, width), BF16), vm((total, width), BF16), vm((rows, width), BF16),
        vm(gshape, F32), vm(gshape, BF16), vm((CHUNKS, width // CHUNKS // 2, width), BF16),
        vm(quarters, F32), vm(quarters, BF16), vm(quarters, BF16),
        vm((mine, width), F32), vm((CHUNKS, mine, width), BF16), vm((CHUNKS, mine, width), BF16),
        vm((members, mine, width), F32),
        dma((8 + CHUNKS,)), dma((CHUNKS + 2,)), dma((4, 2)), dma((4, 2)),
        dma((CHUNKS,)), dma((CHUNKS,)), dma((CHUNKS, members)), dma((CHUNKS, members)),
        dma((CHUNKS,)), dma((CHUNKS,)), dma((members,)), dma((members,)),
    ]
    hbm = pl.BlockSpec(memory_space=pl.ANY)
    smem = pl.BlockSpec(memory_space=pltpu.SMEM)
    result, grid_grad, grad = pl.pallas_call(
        functools.partial(kernel, bands, members, scale, fused),
        out_shape=(
            jax.ShapeDtypeStruct(mesh_latent.shape, BF16),
            jax.ShapeDtypeStruct(grid_latent.shape, BF16),
            jax.ShapeDtypeStruct(last, F32),
        ),
        in_specs=[hbm, hbm, hbm, hbm, smem, hbm, smem, hbm, hbm, hbm],
        out_specs=(hbm, hbm, hbm),
        scratch_shapes=scratch,
        compiler_params=pltpu.CompilerParams(
            collective_id=0, has_side_effects=True, vmem_limit_bytes=40 * 1024 * 1024
        ),
    )(
        grid_latent, mesh_latent, cotangent, edge_weights, edge_targets, mesh_weights, mesh_sources,
        encode_weight, aggregate_weight, process_weight,
    )
    if fused:
        grad = grad.reshape(share, width)
    else:
        summed = lax.psum(grad.reshape(width, width), ("ens", "grid"))
        grad = lax.dynamic_slice_in_dim(summed, lax.axis_index("grid") * share, share, 0)
    return result, grid_grad, grad


def solution(mesh):
    return jax.shard_map(
        functools.partial(on_device, mesh.shape["grid"], mesh.shape["ens"]),
        mesh=mesh,
        in_specs=(
            P("ens", "grid", None),
            P("ens", "grid", None),
            P("ens", "grid", None),
            P("grid", None, None, None),
            P("grid", None),
            P("grid", None, None, None),
            P("grid", None),
            P(),
            P(),
            P(),
        ),
        out_specs=(P("ens", "grid", None), P("ens", "grid", None), P("grid", None)),
        check_vma=False,
    )
```

time: 203 us -> 48.7 us (0.24)
  waiting for transfers between devices: 139 us -> 0 us
  Pallas kernels: 0 us -> 36.6 us
  starting transfers between devices: 26.1 us -> 0 us
  matrix products: 14.9 us -> 0 us
  between operations: 14.4 us -> 0.66 us
  local copies, waits for them, and re-layouts: 6.56 us -> 11.1 us
  other arithmetic: 2.1 us -> 0 us
    psum x1 -> x0, waiting for transfers between devices: 132 us -> none  [on_device(): summed = lax.psum(partial_grad, ('ens', 'grid'))]
    pallas_call x0 -> x1, Pallas kernels: none -> 36.6 us  [on_device(): pl.pallas_call(functools.partial(kernel, bands, members, scale, fused), o...]
    ppermute x8 -> x0, starting transfers between devices: 26 us -> none  [the longest x2 12.2 us: with_halo(): lax.ppermute(tail, axis, [(i, (i + 1) % count) for i in range(ends)])]
    dot_general x13 -> x0, matrix products: 14.9 us -> none  [the longest x1 3.35 us: on_device(): encoded = jnp.dot(grid_x, encode_weight, preferred_element_type=jnp.float32)]
    unnamed x27 -> x22, local copies, waits for them, and re-layouts: 2.24 us -> 11.1 us
    ppermute x8 -> x0, waiting for transfers between devices: 6.72 us -> none  [the longest x4 4.83 us: passed_along(): lax.ppermute(value, axis, [(source, source + steps) for source in range(i...]
    dot_general x3 -> x0, local copies, waits for them, and re-layouts: 3.22 us -> none  [the longest x1 2.95 us: on_device(): jnp.einsum('bkac,bcd->bkad', edge_weights, messages, preferred_element_ty...]
  transfers between devices with their start and end apart: 9 -> 0, of which waited for: 5 -> 0; matrix products, arithmetic and copies ran while one was open for 1% -> 0% of each run, Pallas kernels for 0% -> 0%
where the time goes in v1:
time: 48.7 us; the launch traced here: 48.3 us
  Pallas kernels  36.6 us (75%)
  local copies, waits for them, and re-layouts  11.1 us (23%)
  between operations  0.66 us (1%)
    pallas_call x1, Pallas kernels, on_device(): pl.pallas_call(functools.partial(kernel, bands, members, scale, fused), o...  36.6 us
    unnamed x22, local copies, waits for them, and re-layouts  11.1 us

profile of v1, /device:TPU:0, one launch (start us, length us, event | category | flops | bytes accessed | tf_op | source)
XLA Modules:
  0.0 48.3 jit_solution(4968927439160647958)
XLA Ops:
  0.6 0.0 copy-start.8
  0.6 0.8 %copy.13.targets = s32[8,2]{1,0:T(8,128)S(1)} copy(s32[8,2]{0,1:T(2,128)} %param.14) | data formatting | bytes 128 | tf_op args[4]
  1.4 0.0 copy-done.8
  1.4 0.0 copy-start
  1.4 1.2 %copy-done = bf16[1,1024,512]{2,1,0:T(8,128)(2,1)S(1)} copy-done((bf16[1,1024,512]{2,1,0:T(8,128)(2,1)S(1)}, bf16[1,1024,512]{2,1,0:T(8,128)(2,1)}, u32[]{:S(2)}) %copy-start) | copy-done | bytes 1048600
  2.6 0.0 copy-start.1
  2.6 1.0 %copy-done.1 = bf16[8,2,128,128]{3,2,1,0:T(8,128)(2,1)S(1)} copy-done((bf16[8,2,128,128]{3,2,1,0:T(8,128)(2,1)S(1)}, bf16[8,2,128,128]{3,2,1,0:T(8,128)(2,1)}, u32[]{:S(2)}) %copy-start.1) | copy-done | bytes 524312
  3.7 0.0 copy-start.2
  3.7 1.0 %copy-done.2 = bf16[512,512]{1,0:T(8,128)(2,1)S(1)} copy-done((bf16[512,512]{1,0:T(8,128)(2,1)S(1)}, bf16[512,512]{1,0:T(8,128)(2,1)}, u32[]{:S(2)}) %copy-start.2) | copy-done | bytes 524312
  4.7 0.0 copy-start.3
  4.7 1.0 %copy-done.3 = bf16[512,512]{1,0:T(8,128)(2,1)S(1)} copy-done((bf16[512,512]{1,0:T(8,128)(2,1)S(1)}, bf16[512,512]{1,0:T(8,128)(2,1)}, u32[]{:S(2)}) %copy-start.3) | copy-done | bytes 524312
  5.8 0.0 copy-start.4
  5.8 1.0 %copy-done.4 = bf16[512,512]{1,0:T(8,128)(2,1)S(1)} copy-done((bf16[512,512]{1,0:T(8,128)(2,1)S(1)}, bf16[512,512]{1,0:T(8,128)(2,1)}, u32[]{:S(2)}) %copy-start.4) | copy-done | bytes 524312
  6.8 0.0 copy-start.5
  6.8 0.9 %copy-done.5 = bf16[1,128,512]{2,1,0:T(8,128)(2,1)S(1)} copy-done((bf16[1,128,512]{2,1,0:T(8,128)(2,1)S(1)}, bf16[1,128,512]{2,1,0:T(8,128)(2,1)}, u32[]{:S(2)}) %copy-start.5) | copy-done | bytes 131096
  7.7 0.0 copy-start.6
  7.7 0.9 %copy-done.6 = bf16[1,128,512]{2,1,0:T(8,128)(2,1)S(1)} copy-done((bf16[1,128,512]{2,1,0:T(8,128)(2,1)S(1)}, bf16[1,128,512]{2,1,0:T(8,128)(2,1)}, u32[]{:S(2)}) %copy-start.6) | copy-done | bytes 131096
  8.6 0.0 copy-start.7
  8.6 0.8 %copy-done.7 = bf16[1,2,128,128]{3,2,1,0:T(8,128)(2,1)S(1)} copy-done((bf16[1,2,128,128]{3,2,1,0:T(8,128)(2,1)S(1)}, bf16[1,2,128,128]{3,2,1,0:T(8,128)(2,1)}, u32[]{:S(2)}) %copy-start.7) | copy-done | bytes 65560
  9.4 36.6 %shard_map.121 = (bf16[1,128,512]{2,1,0:T(8,128)(2,1)S(1)}, bf16[1,1024,512]{2,1,0:T(8,128)(2,1)S(1)}, f32[4,16,512]{2,1,0:T(8,128)S(1)}) custom-call(bf16[1,1024,512]{2,1,0:T(8,128)(2,1)S(1)} %copy-done, bf16[1,128,512]{2,1,0:T(8,128)(2,1)S(1)} %copy-done.5, bf16[1,128,512]{2,1,0:T(8,128)(2,1)S(1)} %copy-done.6, bf16[8,2,128,128]{3,2,1,0:T(8,128)(2,1)S(1)} %copy-done.1, ...), custom_call_target="tpu_custom_call" | custom-call | tf_op jit(solution)/shard_map/pallas_call | solution.py:347
  46.0 0.7 %copy.17 = bf16[1,128,512]{2,1,0:T(8,128)(2,1)} copy(bf16[1,128,512]{2,1,0:T(8,128)(2,1)S(1)} %get-tuple-element.12) | data formatting | bytes 262144
  46.7 1.0 %copy.18 = bf16[1,1024,512]{2,1,0:T(8,128)(2,1)} copy(bf16[1,1024,512]{2,1,0:T(8,128)(2,1)S(1)} %get-tuple-element.13) | data formatting | bytes 2097152
  47.6 0.7 %copy.19 = f32[64,512]{1,0:T(8,128)} copy(f32[64,512]{1,0:T(8,128)S(1)} %bitcast.1) | data formatting | bytes 262144
Async XLA Ops:
  0.6 0.8 %copy-start.8 = (s32[1,2]{1,0:T(1,128)S(1)}, s32[1,2]{1,0:T(1,128)}, u32[]{:S(2)}) copy-start(s32[1,2]{1,0:T(1,128)} %sources.1) | copy-start | bytes 28
  1.4 1.2 %copy-start = (bf16[1,1024,512]{2,1,0:T(8,128)(2,1)S(1)}, bf16[1,1024,512]{2,1,0:T(8,128)(2,1)}, u32[]{:S(2)}) copy-start(bf16[1,1024,512]{2,1,0:T(8,128)(2,1)} %x_h.1) | copy-start | bytes 3145732
  2.6 1.0 %copy-start.1 = (bf16[8,2,128,128]{3,2,1,0:T(8,128)(2,1)S(1)}, bf16[8,2,128,128]{3,2,1,0:T(8,128)(2,1)}, u32[]{:S(2)}) copy-start(bf16[8,2,128,128]{3,2,1,0:T(8,128)(2,1)} %edge_h.1) | copy-start | bytes 1572868
  3.7 1.0 %copy-start.2 = (bf16[512,512]{1,0:T(8,128)(2,1)S(1)}, bf16[512,512]{1,0:T(8,128)(2,1)}, u32[]{:S(2)}) copy-start(bf16[512,512]{1,0:T(8,128)(2,1)} %enc_w_h.1) | copy-start | bytes 1572868
  4.7 1.0 %copy-start.3 = (bf16[512,512]{1,0:T(8,128)(2,1)S(1)}, bf16[512,512]{1,0:T(8,128)(2,1)}, u32[]{:S(2)}) copy-start(bf16[512,512]{1,0:T(8,128)(2,1)} %agg_w_h.1) | copy-start | bytes 1572868
  5.8 1.0 %copy-start.4 = (bf16[512,512]{1,0:T(8,128)(2,1)S(1)}, bf16[512,512]{1,0:T(8,128)(2,1)}, u32[]{:S(2)}) copy-start(bf16[512,512]{1,0:T(8,128)(2,1)} %proc_w_h.1) | copy-start | bytes 1572868
  6.8 0.9 %copy-start.5 = (bf16[1,128,512]{2,1,0:T(8,128)(2,1)S(1)}, bf16[1,128,512]{2,1,0:T(8,128)(2,1)}, u32[]{:S(2)}) copy-start(bf16[1,128,512]{2,1,0:T(8,128)(2,1)} %mesh_h.1) | copy-start | bytes 393220
  7.7 0.9 %copy-start.6 = (bf16[1,128,512]{2,1,0:T(8,128)(2,1)S(1)}, bf16[1,128,512]{2,1,0:T(8,128)(2,1)}, u32[]{:S(2)}) copy-start(bf16[1,128,512]{2,1,0:T(8,128)(2,1)} %cot_h.1) | copy-start | bytes 393220
  8.6 0.8 %copy-start.7 = (bf16[1,2,128,128]{3,2,1,0:T(8,128)(2,1)S(1)}, bf16[1,2,128,128]{3,2,1,0:T(8,128)(2,1)}, u32[]{:S(2)}) copy-start(bf16[1,2,128,128]{3,2,1,0:T(8,128)(2,1)} %mweight_h.1) | copy-start | bytes 196612

commit v2 on v1

--- a/solution.py
+++ b/solution.py
@@ -32,13 +32,13 @@
 
 def kernel(
     bands, members, scale, fused,
-    x_h, mesh_h, cot_h, edge_h, targets, mweight_h, sources, enc_w_h, agg_w_h, proc_w_h,
+    x_h, mesh_h, cot_h, edge_h, targets_h, mweight_h, sources_h, enc_w_h, agg_w_h, proc_w_h,
     result_h, grid_h, final_h,
-    x, mesh, cot, edge, mweight, enc_w, agg_w, proc_w,
+    x, mesh, cot, edge, targets, mweight, sources, enc_w, agg_w, proc_w,
     wide, wide_own_t, wide_side_t, near, near_t, x_t,
     encoded, messages, panel_out, panel_in, upd, upd_in, push_out, push_in, agg, agg_in,
     own_grad, enc_delta, grid_out, result,
-    part, part_out, pair_in, quarter, quarter_out, ens_in, summed, summed_out, z_in, final,
+    part, part_out, pair_in, quarter, quarter_out, ens_in, summed, summed_out, z_in, final, final_out,
     in_sem, out_sem, halo_send, halo_recv, a_send, a_recv, b_send, b_recv, c_send, c_recv, d_send, d_recv,
 ):
     me = lax.axis_index("grid")
@@ -63,6 +63,7 @@
         copy.start()
         return copy
 
+    targets_copy = local(targets_h, targets, in_sem.at[7])
     edge_copy = local(edge_h, edge, in_sem.at[0])
     enc_copy = local(enc_w_h, enc_w, in_sem.at[1])
     x_copies = [
@@ -74,6 +75,7 @@
     mweight_copy = local(mweight_h.at[0], mweight, in_sem.at[4])
     proc_copy = local(proc_w_h, proc_w, in_sem.at[5])
     cot_copy = local(cot_h.at[0], cot, in_sem.at[6])
+    sources_copy = local(sources_h, sources, in_sem.at[8 + CHUNKS])
 
     barrier = pltpu.get_barrier_semaphore()
 
@@ -95,12 +97,13 @@
         for ref in (panel_in, upd_in, push_in, agg_in):
             ref[slot] = jnp.zeros(ref.shape[1:], ref.dtype)
 
+    targets_copy.wait()
     edge_copy.wait()
     for b in range(blocks):
         first = edge[b, 0].astype(F32)
         second = edge[b, 1].astype(F32)
         for j in range(3):
-            hit = [jnp.where(targets[b, k] - me + 1 == j, 1.0, 0.0).astype(F32) for k in range(2)]
+            hit = [jnp.where(targets[k, b] - me + 1 == j, 1.0, 0.0).astype(F32) for k in range(2)]
             wide[j, :, b * rows:(b + 1) * rows] = (first * hit[0] + second * hit[1]).astype(BF16)
 
     enc_copy.wait()
@@ -143,11 +146,7 @@
     for i in range(CHUNKS):
         span = pl.ds(i * step, step)
         encoded[span] = slope_of(encoded[span])
-    for b in range(blocks):
-        span = pl.ds(b * rows, rows)
-        wide_own_t[span] = wide[1, :, b * rows:(b + 1) * rows].T
-        wide_side_t[span, 0:rows] = wide[0, :, b * rows:(b + 1) * rows].T
-        wide_side_t[span, rows:2 * rows] = wide[2, :, b * rows:(b + 1) * rows].T
+    sources_copy.wait()
     mweight_copy.wait()
     first = mweight[0].astype(F32)
     second = mweight[1].astype(F32)
@@ -170,8 +169,12 @@
     processed = dot(near[1], updated)
     mesh_slope = mesh_sig * (1.0 + mesh_pre * (1.0 - mesh_sig))
     deep = width // CHUNKS
-    for i in range(CHUNKS):
-        x_t[i] = x[:, i * deep:(i + 1) * deep].T
+    for b in range(blocks):
+        span = pl.ds(b * rows, rows)
+        wide_own_t[span] = wide[1, :, b * rows:(b + 1) * rows].T
+        wide_side_t[span, 0:rows] = wide[0, :, b * rows:(b + 1) * rows].T
+        wide_side_t[span, rows:2 * rows] = wide[2, :, b * rows:(b + 1) * rows].T
+    x_t[0] = x[:, 0:deep].T
     proc_copy.wait()
     cot_copy.wait()
     upstream = cot[...].astype(F32)
@@ -193,6 +196,9 @@
     result[...] = (upd[...].astype(F32) + proc_pre * proc_sig).astype(BF16)
     result_copy = local(result, result_h.at[0], out_sem.at[CHUNKS])
 
+    x_t[1] = x[:, deep:2 * deep].T
+    x_t[2] = x[:, 2 * deep:3 * deep].T
+
     received(2, push_in)
     mesh_grad = mesh_grad + push_in[0].astype(F32) + push_in[1].astype(F32)
     agg_grad = dot_t((mesh_grad * mesh_slope).astype(BF16), agg_w[...]).astype(BF16)
@@ -201,6 +207,8 @@
     for i in range(CHUNKS):
         span = pl.ds(i * step, step)
         own_grad[span] = dot(wide_own_t[span], agg_grad)
+
+    x_t[3] = x[:, 3 * deep:4 * deep].T
 
     received(3, agg_in)
     sides = agg_in[...].reshape(2 * rows, width)
@@ -283,12 +291,13 @@
         for d in range(1, levels):
             along(d, True).wait_recv()
             value = value + z_in[lax.rem(level + d, levels)].astype(F32)
-        final[ens] = value
+        final[ens] = value.astype(BF16)
         for d in range(1, members):
             gather(d, False).start()
         for d in range(1, members):
             gather(d, True).wait_recv()
-        final_copy = local(final, final_h, out_sem.at[CHUNKS + 1])
+        final_out[...] = final[...].astype(F32)
+        final_copy = local(final_out, final_h, out_sem.at[CHUNKS + 1])
         for z in order:
             pair(z).wait_send()
             for d in range(1, members):
@@ -304,6 +313,15 @@
     for copy in grid_copies:
         copy.wait()
     final_copy.wait()
+
+
+def leave(result, grid_grad, grad, result_out, grid_out, grad_out, sem):
+    pairs = ((grid_grad, grid_out), (result, result_out), (grad, grad_out))
+    copies = [pltpu.make_async_copy(src, dst, sem.at[i]) for i, (src, dst) in enumerate(pairs)]
+    for copy in copies:
+        copy.start()
+    for copy in copies:
+        copy.wait()
 
 
 def on_device(
@@ -326,7 +344,9 @@
     quarters = (CHUNKS, members, mine, width)
     scratch = [
         vm((total, width), BF16), vm((rows, width), BF16), vm((rows, width), BF16),
-        vm(edge_weights.shape, BF16), vm(mesh_weights.shape[1:], BF16),
+        vm(edge_weights.shape, BF16),
+        pltpu.SMEM(edge_targets.shape[::-1], jnp.int32), vm(mesh_weights.shape[1:], BF16),
+        pltpu.SMEM(mesh_sources.shape, jnp.int32),
         vm((width, width), BF16), vm((width, width), BF16), vm((width, width), BF16),
         vm((3, rows, total), BF16), vm((total, rows), BF16), vm((total, 2 * rows), BF16),
         vm((3, rows, rows), BF16), vm((3, rows, rows), BF16), vm((CHUNKS, width // CHUNKS, total), BF16),
@@ -337,13 +357,13 @@
         vm(gshape, F32), vm(gshape, BF16), vm((CHUNKS, width // CHUNKS // 2, width), BF16),
         vm(quarters, F32), vm(quarters, BF16), vm(quarters, BF16),
         vm((mine, width), F32), vm((CHUNKS, mine, width), BF16), vm((CHUNKS, mine, width), BF16),
-        vm((members, mine, width), F32),
-        dma((8 + CHUNKS,)), dma((CHUNKS + 2,)), dma((4, 2)), dma((4, 2)),
+        vm((members, mine, width), BF16), vm((members, mine, width), F32),
+        dma((9 + CHUNKS,)), dma((CHUNKS + 2,)), dma((4, 2)), dma((4, 2)),
         dma((CHUNKS,)), dma((CHUNKS,)), dma((CHUNKS, members)), dma((CHUNKS, members)),
         dma((CHUNKS,)), dma((CHUNKS,)), dma((members,)), dma((members,)),
     ]
-    hbm = pl.BlockSpec(memory_space=pl.ANY)
-    smem = pl.BlockSpec(memory_space=pltpu.SMEM)
+    hbm = pl.BlockSpec(memory_space=pltpu.HBM)
+    anywhere = pl.BlockSpec(memory_space=pl.ANY)
     result, grid_grad, grad = pl.pallas_call(
         functools.partial(kernel, bands, members, scale, fused),
         out_shape=(
@@ -351,17 +371,25 @@
             jax.ShapeDtypeStruct(grid_latent.shape, BF16),
             jax.ShapeDtypeStruct(last, F32),
         ),
-        in_specs=[hbm, hbm, hbm, hbm, smem, hbm, smem, hbm, hbm, hbm],
-        out_specs=(hbm, hbm, hbm),
+        in_specs=[hbm] * 10,
+        out_specs=(anywhere,) * 3,
         scratch_shapes=scratch,
         compiler_params=pltpu.CompilerParams(
-            collective_id=0, has_side_effects=True, vmem_limit_bytes=40 * 1024 * 1024
+            collective_id=0, has_side_effects=True, vmem_limit_bytes=63 * 1024 * 1024
         ),
     )(
-        grid_latent, mesh_latent, cotangent, edge_weights, edge_targets, mesh_weights, mesh_sources,
+        grid_latent, mesh_latent, cotangent, edge_weights, edge_targets.T, mesh_weights, mesh_sources,
         encode_weight, aggregate_weight, process_weight,
     )
     if fused:
+        result, grid_grad, grad = pl.pallas_call(
+            leave,
+            out_shape=tuple(jax.ShapeDtypeStruct(a.shape, a.dtype) for a in (result, grid_grad, grad)),
+            in_specs=[anywhere] * 3,
+            out_specs=(hbm,) * 3,
+            scratch_shapes=[dma((3,))],
+            compiler_params=pltpu.CompilerParams(vmem_limit_bytes=63 * 1024 * 1024),
+        )(result, grid_grad, grad)
         grad = grad.reshape(share, width)
     else:
         summed = lax.psum(grad.reshape(width, width), ("ens", "grid"))

time: 48.7 us -> 77.6 us (1.59)
  Pallas kernels: 36.6 us -> 76.8 us
  local copies, waits for them, and re-layouts: 11.1 us -> 0 us
    pallas_call x0 -> x1, Pallas kernels: none -> 40.8 us  [on_device(): pl.pallas_call(leave, out_shape=tuple((jax.ShapeDtypeStruct(a.shape, a.dt...]
    unnamed x22 -> x0, local copies, waits for them, and re-layouts: 11.1 us -> none
where the time goes in v2:
time: 77.6 us; the launch traced here: 77.4 us
  Pallas kernels  76.8 us (99%)
    pallas_call x1, Pallas kernels, on_device(): pl.pallas_call(leave, out_shape=tuple((jax.ShapeDtypeStruct(a.shape, a.dt...  40.8 us
    pallas_call x1, Pallas kernels, on_device(): pl.pallas_call(functools.partial(kernel, bands, members, scale, fused), o...  36 us

profile of v2, /device:TPU:0, one launch (start us, length us, event | category | flops | bytes accessed | tf_op | source)
XLA Modules:
  0.0 77.4 jit_solution(15830081888520630800)
XLA Ops:
  0.6 36.0 %shard_map.121 = (bf16[1,128,512]{2,1,0:T(8,128)(2,1)}, bf16[1,1024,512]{2,1,0:T(8,128)(2,1)}, f32[4,16,512]{2,1,0:T(8,128)}) custom-call(bf16[1,1024,512]{2,1,0:T(8,128)(2,1)} %x_h.1, bf16[1,128,512]{2,1,0:T(8,128)(2,1)} %mesh_h.1, bf16[1,128,512]{2,1,0:T(8,128)(2,1)} %cot_h.1, bf16[8,2,128,128]{3,2,1,0:T(8,128)(2,1)} %edge_h.1, s32[2,8]{1,0:T(2,128)} %bitcast.2, ...), custom_call_target="tpu_custom_call" | custom-call | tf_op jit(solution)/shard_map/pallas_call | solution.py:367
  36.6 40.8 %shard_map.122 = (bf16[1,128,512]{2,1,0:T(8,128)(2,1)}, bf16[1,1024,512]{2,1,0:T(8,128)(2,1)}, f32[4,16,512]{2,1,0:T(8,128)}) custom-call(bf16[1,128,512]{2,1,0:T(8,128)(2,1)} %get-tuple-element.9.result, bf16[1,1024,512]{2,1,0:T(8,128)(2,1)} %get-tuple-element.10.grid_grad, f32[4,16,512]{2,1,0:T(8,128)} %get-tuple-element.11.grad), custom_call_target="tpu_custom_call" | custom-call | tf_op jit(solution)/shard_map/pallas_call | solution.py:385

commit v3 on v2

--- a/solution.py
+++ b/solution.py
@@ -11,6 +11,7 @@
 F32 = jnp.float32
 BF16 = jnp.bfloat16
 CHUNKS = 4
+HALVES = 2
 
 
 def sigmoid(value):
@@ -36,8 +37,8 @@
     result_h, grid_h, final_h,
     x, mesh, cot, edge, targets, mweight, sources, enc_w, agg_w, proc_w,
     wide, wide_own_t, wide_side_t, near, near_t, x_t,
-    encoded, messages, panel_out, panel_in, upd, upd_in, push_out, push_in, agg, agg_in,
-    own_grad, enc_delta, grid_out, result,
+    encoded, panels, panel_out, panel_in, upd, upd_in, push_out, push_in, agg, agg_in,
+    mesh_slope, mesh_grad, own_grad, enc_delta, grid_out, result,
     part, part_out, pair_in, quarter, quarter_out, ens_in, summed, summed_out, z_in, final, final_out,
     in_sem, out_sem, halo_send, halo_recv, a_send, a_recv, b_send, b_recv, c_send, c_recv, d_send, d_recv,
 ):
@@ -104,48 +105,53 @@
         second = edge[b, 1].astype(F32)
         for j in range(3):
             hit = [jnp.where(targets[k, b] - me + 1 == j, 1.0, 0.0).astype(F32) for k in range(2)]
-            wide[j, :, b * rows:(b + 1) * rows] = (first * hit[0] + second * hit[1]).astype(BF16)
-
-    enc_copy.wait()
-    for i in range(CHUNKS):
-        x_copies[i].wait()
-        span = pl.ds(i * step, step)
-        value = dot(x[span], enc_w[...])
-        encoded[span] = value
-        messages[span] = (value * sigmoid(value)).astype(BF16)
-
-    def halo(turn, source, landing, off):
+            wide[j * rows:(j + 1) * rows, b * rows:(b + 1) * rows] = (first * hit[0] + second * hit[1]).astype(BF16)
+
+    half = width // HALVES
+    cols = [slice(h * half, (h + 1) * half) for h in range(HALVES)]
+
+    def halo(turn, h, source, landing, off):
         slot = (1 - off) // 2
         return pltpu.make_async_remote_copy(
-            src_ref=source,
-            dst_ref=landing.at[slot],
-            send_sem=halo_send.at[turn, slot],
-            recv_sem=halo_recv.at[turn, slot],
+            src_ref=source.at[:, cols[h]],
+            dst_ref=landing.at[slot, :, cols[h]],
+            send_sem=halo_send.at[turn, slot, h],
+            recv_sem=halo_recv.at[turn, slot, h],
             device_id={"grid": me + off},
             device_id_type=MESH,
         )
 
-    def received(turn, landing):
-        act = lambda off: halo(turn, landing.at[(1 - off) // 2], landing, off).wait_recv()
+    def received(turn, h, landing):
+        act = lambda off: halo(turn, h, landing.at[(1 - off) // 2], landing, off).wait_recv()
         act(far)
         pl.when(far_there)(lambda: act(-far))
 
-    def sent(turn, landing):
-        both(lambda off: halo(turn, landing.at[(1 - off) // 2], landing, off).wait_send())
-
-    pl.semaphore_wait(barrier, expected)
-    for off, there in ((far, far_there), (-far, None)):
-        panel_out[(1 - off) // 2] = dot(wide[1 + off], messages[...]).astype(BF16)
-        go = functools.partial(halo, 0, panel_out.at[(1 - off) // 2], panel_in, off)
-        if there is None:
-            go().start()
-        else:
-            pl.when(there)(lambda: go().start())
-
-    own_panel = dot(wide[1], messages[...])
-    for i in range(CHUNKS):
-        span = pl.ds(i * step, step)
+    def sent(turn, h, landing):
+        both(lambda off: halo(turn, h, landing.at[(1 - off) // 2], landing, off).wait_send())
+
+    enc_copy.wait()
+    for h in range(HALVES):
+        for i in range(CHUNKS):
+            if h == 0:
+                x_copies[i].wait()
+            span = pl.ds(i * step, step)
+            value = dot(x[span], enc_w[:, cols[h]])
+            encoded[span, cols[h]] = value
+            message = (value * sigmoid(value)).astype(BF16)
+            term = dot(wide[:, i * step:(i + 1) * step], message)
+            panels[:, cols[h]] = term if i == 0 else panels[:, cols[h]] + term
+        if h == 0:
+            pl.semaphore_wait(barrier, expected)
+        for off in (far, -far):
+            panel_out[(1 - off) // 2, :, cols[h]] = panels[pl.ds((1 + off) * rows, rows), cols[h]].astype(BF16)
+        both(lambda off: halo(0, h, panel_out.at[(1 - off) // 2], panel_in, off).start())
+
+    def slopes(i, carry):
+        span = pl.ds(pl.multiple_of(i * 64, 64), 64)
         encoded[span] = slope_of(encoded[span])
+        return carry
+
+    lax.fori_loop(0, total // 64, slopes, 0)
     sources_copy.wait()
     mweight_copy.wait()
     first = mweight[0].astype(F32)
@@ -158,64 +164,97 @@
     mesh_copy.wait()
     agg_copy.wait()
 
-    received(0, panel_in)
-    aggregated = own_panel + panel_in[0].astype(F32) + panel_in[1].astype(F32)
-    mesh_pre = dot(aggregated.astype(BF16), agg_w[...])
-    mesh_sig = sigmoid(mesh_pre)
-    updated = (mesh[...].astype(F32) + mesh_pre * mesh_sig).astype(BF16)
-    upd[...] = updated
-    both(lambda off: halo(1, upd, upd_in, off).start())
-
-    processed = dot(near[1], updated)
-    mesh_slope = mesh_sig * (1.0 + mesh_pre * (1.0 - mesh_sig))
+    partial = [0.0] * HALVES
+    for h in range(HALVES):
+        received(0, h, panel_in)
+        landed = panels[rows:2 * rows, cols[h]]
+        for slot in range(2):
+            landed = landed + panel_in[slot, :, cols[h]].astype(F32)
+        landed = landed.astype(BF16)
+        for n in range(HALVES):
+            partial[n] = partial[n] + dot(landed, agg_w[cols[h], cols[n]])
+            if h == HALVES - 1:
+                pre = partial[n]
+                sig = sigmoid(pre)
+                upd[:, cols[n]] = (mesh[:, cols[n]].astype(F32) + pre * sig).astype(BF16)
+                both(lambda off: halo(1, n, upd, upd_in, off).start())
+                mesh_slope[:, cols[n]] = sig * (1.0 + pre * (1.0 - sig))
+
+    own = dot(near[1], upd[...])
+
+    def turn_edges(b, carry):
+        span = pl.ds(pl.multiple_of(b * rows, rows), rows)
+        wide_own_t[span] = wide[rows:2 * rows, span].T
+        wide_side_t[span, 0:rows] = wide[0:rows, span].T
+        wide_side_t[span, rows:2 * rows] = wide[2 * rows:3 * rows, span].T
+        return carry
+
     deep = width // CHUNKS
-    for b in range(blocks):
-        span = pl.ds(b * rows, rows)
-        wide_own_t[span] = wide[1, :, b * rows:(b + 1) * rows].T
-        wide_side_t[span, 0:rows] = wide[0, :, b * rows:(b + 1) * rows].T
-        wide_side_t[span, rows:2 * rows] = wide[2, :, b * rows:(b + 1) * rows].T
-    x_t[0] = x[:, 0:deep].T
+
+    def turn_x(i):
+        def body(b, carry):
+            span = pl.ds(pl.multiple_of(b * rows, rows), rows)
+            x_t[i, :, span] = x[span, i * deep:(i + 1) * deep].T
+            return carry
+
+        lax.fori_loop(0, blocks, body, 0)
+
+    lax.fori_loop(0, blocks, turn_edges, 0)
+    turn_x(0)
     proc_copy.wait()
     cot_copy.wait()
-    upstream = cot[...].astype(F32)
-
-    received(1, upd_in)
-    processed = processed + dot(near[0], upd_in[0]) + dot(near[2], upd_in[1])
-    proc_pre = dot(processed.astype(BF16), proc_w[...])
+
+    proc_pre = 0.0
+    for h in range(HALVES):
+        received(1, h, upd_in)
+        mixed = own[:, cols[h]] + dot(near[0], upd_in[0, :, cols[h]]) + dot(near[2], upd_in[1, :, cols[h]])
+        proc_pre = proc_pre + dot(mixed.astype(BF16), proc_w[cols[h], :])
     proc_sig = sigmoid(proc_pre)
     proc_slope = proc_sig * (1.0 + proc_pre * (1.0 - proc_sig))
-    proc_back = dot_t((upstream * proc_slope).astype(BF16), proc_w[...]).astype(BF16)
-    for off, there in ((far, far_there), (-far, None)):
-        push_out[(1 - off) // 2] = dot(near_t[1 + off], proc_back).astype(BF16)
-        go = functools.partial(halo, 2, push_out.at[(1 - off) // 2], push_in, off)
-        if there is None:
-            go().start()
-        else:
-            pl.when(there)(lambda: go().start())
-    mesh_grad = upstream + dot(near_t[1], proc_back)
+    upstream = cot[...].astype(F32)
+    proc_delta = (upstream * proc_slope).astype(BF16)
+    backs = []
+    for n in range(HALVES):
+        back = dot_t(proc_delta, proc_w[cols[n], :]).astype(BF16)
+        for off in (far, -far):
+            push_out[(1 - off) // 2, :, cols[n]] = dot(near_t[1 + off], back).astype(BF16)
+        both(lambda off: halo(2, n, push_out.at[(1 - off) // 2], push_in, off).start())
+        backs.append(back)
+    for n in range(HALVES):
+        mesh_grad[:, cols[n]] = upstream[:, cols[n]] + dot(near_t[1], backs[n])
     result[...] = (upd[...].astype(F32) + proc_pre * proc_sig).astype(BF16)
     result_copy = local(result, result_h.at[0], out_sem.at[CHUNKS])
-
-    x_t[1] = x[:, deep:2 * deep].T
-    x_t[2] = x[:, 2 * deep:3 * deep].T
-
-    received(2, push_in)
-    mesh_grad = mesh_grad + push_in[0].astype(F32) + push_in[1].astype(F32)
-    agg_grad = dot_t((mesh_grad * mesh_slope).astype(BF16), agg_w[...]).astype(BF16)
-    agg[...] = agg_grad
-    both(lambda off: halo(3, agg, agg_in, off).start())
-    for i in range(CHUNKS):
-        span = pl.ds(i * step, step)
-        own_grad[span] = dot(wide_own_t[span], agg_grad)
-
-    x_t[3] = x[:, 3 * deep:4 * deep].T
-
-    received(3, agg_in)
-    sides = agg_in[...].reshape(2 * rows, width)
-    for i in range(CHUNKS):
-        span = pl.ds(i * step, step)
-        grad = own_grad[span] + dot(wide_side_t[span], sides)
-        enc_delta[span] = (grad * encoded[span]).astype(BF16)
+    turn_x(1)
+    turn_x(2)
+
+    partial = [0.0] * HALVES
+    for h in range(HALVES):
+        received(2, h, push_in)
+        landed = mesh_grad[:, cols[h]]
+        for slot in range(2):
+            landed = landed + push_in[slot, :, cols[h]].astype(F32)
+        landed = (landed * mesh_slope[:, cols[h]]).astype(BF16)
+        for n in range(HALVES):
+            partial[n] = partial[n] + dot_t(landed, agg_w[cols[n], cols[h]])
+            if h == HALVES - 1:
+                agg[:, cols[n]] = partial[n].astype(BF16)
+                both(lambda off: halo(3, n, agg, agg_in, off).start())
+
+    def own_part(i, carry):
+        span = pl.ds(pl.multiple_of(i * step, step), step)
+        own_grad[span] = dot(wide_own_t[span], agg[...])
+        return carry
+
+    lax.fori_loop(0, CHUNKS, own_part, 0)
+    turn_x(3)
+
+    for h in range(HALVES):
+        received(3, h, agg_in)
+        sides = agg_in[:, :, cols[h]].reshape(2 * rows, half)
+        for i in range(CHUNKS):
+            span = pl.ds(i * step, step)
+            grad = own_grad[span, cols[h]] + dot(wide_side_t[span], sides)
+            enc_delta[span, cols[h]] = (grad * encoded[span, cols[h]]).astype(BF16)
 
     def grid_part(i):
         span = pl.ds(i * step, step)
@@ -308,19 +347,28 @@
             gather(d, False).wait_send()
 
     for turn, landing in enumerate((panel_in, upd_in, push_in, agg_in)):
-        sent(turn, landing)
+        for h in range(HALVES):
+            sent(turn, h, landing)
     result_copy.wait()
     for copy in grid_copies:
         copy.wait()
     final_copy.wait()
 
 
-def leave(result, grid_grad, grad, result_out, grid_out, grad_out, sem):
-    pairs = ((grid_grad, grid_out), (result, result_out), (grad, grad_out))
-    copies = [pltpu.make_async_copy(src, dst, sem.at[i]) for i, (src, dst) in enumerate(pairs)]
-    for copy in copies:
+def leave(result, grid_grad, grad, result_out, grid_out, grad_out, one, two, three, in_sem, out_sem):
+    step = grid_grad.shape[1] // CHUNKS
+    moves = [(result, one, result_out), (grad, three, grad_out)]
+    for i in range(CHUNKS):
+        span = pl.ds(i * step, step)
+        moves.append((grid_grad.at[:, span], two.at[:, span], grid_out.at[:, span]))
+    arriving = [pltpu.make_async_copy(a, b, in_sem.at[i]) for i, (a, b, c) in enumerate(moves)]
+    leaving = [pltpu.make_async_copy(b, c, out_sem.at[i]) for i, (a, b, c) in enumerate(moves)]
+    for copy in arriving:
         copy.start()
-    for copy in copies:
+    for first, second in zip(arriving, leaving):
+        first.wait()
+        second.start()
+    for copy in leaving:
         copy.wait()
 
 
@@ -348,17 +396,18 @@
         pltpu.SMEM(edge_targets.shape[::-1], jnp.int32), vm(mesh_weights.shape[1:], BF16),
         pltpu.SMEM(mesh_sources.shape, jnp.int32),
         vm((width, width), BF16), vm((width, width), BF16), vm((width, width), BF16),
-        vm((3, rows, total), BF16), vm((total, rows), BF16), vm((total, 2 * rows), BF16),
+        vm((3 * rows, total), BF16), vm((total, rows), BF16), vm((total, 2 * rows), BF16),
         vm((3, rows, rows), BF16), vm((3, rows, rows), BF16), vm((CHUNKS, width // CHUNKS, total), BF16),
-        vm((total, width), F32), vm((total, width), BF16),
+        vm((total, width), F32), vm((3 * rows, width), F32),
         vm(panel, BF16), vm(panel, BF16), vm((rows, width), BF16), vm(panel, BF16),
         vm(panel, BF16), vm(panel, BF16), vm((rows, width), BF16), vm(panel, BF16),
+        vm((rows, width), F32), vm((rows, width), F32),
         vm((total, width), F32), vm((total, width), BF16), vm((total, width), BF16), vm((rows, width), BF16),
         vm(gshape, F32), vm(gshape, BF16), vm((CHUNKS, width // CHUNKS // 2, width), BF16),
         vm(quarters, F32), vm(quarters, BF16), vm(quarters, BF16),
         vm((mine, width), F32), vm((CHUNKS, mine, width), BF16), vm((CHUNKS, mine, width), BF16),
         vm((members, mine, width), BF16), vm((members, mine, width), F32),
-        dma((9 + CHUNKS,)), dma((CHUNKS + 2,)), dma((4, 2)), dma((4, 2)),
+        dma((9 + CHUNKS,)), dma((CHUNKS + 2,)), dma((4, 2, HALVES)), dma((4, 2, HALVES)),
         dma((CHUNKS,)), dma((CHUNKS,)), dma((CHUNKS, members)), dma((CHUNKS, members)),
         dma((CHUNKS,)), dma((CHUNKS,)), dma((members,)), dma((members,)),
     ]
@@ -387,7 +436,7 @@
             out_shape=tuple(jax.ShapeDtypeStruct(a.shape, a.dtype) for a in (result, grid_grad, grad)),
             in_specs=[anywhere] * 3,
             out_specs=(hbm,) * 3,
-            scratch_shapes=[dma((3,))],
+            scratch_shapes=[vm(a.shape, a.dtype) for a in (result, grid_grad, grad)] + [dma((2 + CHUNKS,))] * 2,
             compiler_params=pltpu.CompilerParams(vmem_limit_bytes=63 * 1024 * 1024),
         )(result, grid_grad, grad)
         grad = grad.reshape(share, width)

time: 77.6 us -> 39 us (0.50)
  Pallas kernels: 76.8 us -> 38.2 us
    pallas_call x1, Pallas kernels: 40.8 us -> 2.15 us  [on_device(): pl.pallas_call(leave, out_shape=tuple((jax.ShapeDtypeStruct(a.shape, a.dt...]
where the time goes in v3:
time: 39 us; the launch traced here: 38.8 us
  Pallas kernels  38.2 us (98%)
  between operations  0.64 us (2%)
    pallas_call x1, Pallas kernels, on_device(): pl.pallas_call(functools.partial(kernel, bands, members, scale, fused), o...  36 us
    pallas_call x1, Pallas kernels, on_device(): pl.pallas_call(leave, out_shape=tuple((jax.ShapeDtypeStruct(a.shape, a.dt...  2.15 us

profile of v3, /device:TPU:0, one launch (start us, length us, event | category | flops | bytes accessed | tf_op | source)
XLA Modules:
  0.0 38.8 jit_solution(393128397657298753)
XLA Ops:
  0.6 36.0 %shard_map.121 = (bf16[1,128,512]{2,1,0:T(8,128)(2,1)}, bf16[1,1024,512]{2,1,0:T(8,128)(2,1)}, f32[4,16,512]{2,1,0:T(8,128)}) custom-call(bf16[1,1024,512]{2,1,0:T(8,128)(2,1)} %x_h.1, bf16[1,128,512]{2,1,0:T(8,128)(2,1)} %mesh_h.1, bf16[1,128,512]{2,1,0:T(8,128)(2,1)} %cot_h.1, bf16[8,2,128,128]{3,2,1,0:T(8,128)(2,1)} %edge_h.1, s32[2,8]{1,0:T(2,128)} %bitcast.2, ...), custom_call_target="tpu_custom_call" | custom-call | tf_op jit(solution)/shard_map/pallas_call | solution.py:416
  36.7 2.1 %shard_map.122 = (bf16[1,128,512]{2,1,0:T(8,128)(2,1)}, bf16[1,1024,512]{2,1,0:T(8,128)(2,1)}, f32[4,16,512]{2,1,0:T(8,128)}) custom-call(bf16[1,128,512]{2,1,0:T(8,128)(2,1)} %get-tuple-element.9.result, bf16[1,1024,512]{2,1,0:T(8,128)(2,1)} %get-tuple-element.10.grid_grad, f32[4,16,512]{2,1,0:T(8,128)} %get-tuple-element.11.grad), custom_call_target="tpu_custom_call" | custom-call | tf_op jit(solution)/shard_map/pallas_call | solution.py:434

commit v4 on v3

--- a/solution.py
+++ b/solution.py
@@ -100,12 +100,18 @@
 
     targets_copy.wait()
     edge_copy.wait()
-    for b in range(blocks):
+
+    def mix_edges(b, carry):
         first = edge[b, 0].astype(F32)
         second = edge[b, 1].astype(F32)
+        span = pl.ds(pl.multiple_of(b * rows, rows), rows)
         for j in range(3):
             hit = [jnp.where(targets[k, b] - me + 1 == j, 1.0, 0.0).astype(F32) for k in range(2)]
-            wide[j * rows:(j + 1) * rows, b * rows:(b + 1) * rows] = (first * hit[0] + second * hit[1]).astype(BF16)
+            wide[j * rows:(j + 1) * rows, span] = (first * hit[0] + second * hit[1]).astype(BF16)
+        return carry
+
+    lax.fori_loop(0, blocks, mix_edges, 0)
+    panels[...] = jnp.zeros_like(panels)
 
     half = width // HALVES
     cols = [slice(h * half, (h + 1) * half) for h in range(HALVES)]
@@ -131,15 +137,19 @@
 
     enc_copy.wait()
     for h in range(HALVES):
-        for i in range(CHUNKS):
-            if h == 0:
-                x_copies[i].wait()
-            span = pl.ds(i * step, step)
+        if h == 0:
+            for copy in x_copies:
+                copy.wait()
+
+        def encode(i, carry):
+            span = pl.ds(pl.multiple_of(i * step, step), step)
             value = dot(x[span], enc_w[:, cols[h]])
             encoded[span, cols[h]] = value
             message = (value * sigmoid(value)).astype(BF16)
-            term = dot(wide[:, i * step:(i + 1) * step], message)
-            panels[:, cols[h]] = term if i == 0 else panels[:, cols[h]] + term
+            panels[:, cols[h]] += dot(wide[:, span], message)
+            return carry
+
+        lax.fori_loop(0, CHUNKS, encode, 0)
         if h == 0:
             pl.semaphore_wait(barrier, expected)
         for off in (far, -far):
@@ -251,21 +261,30 @@
     for h in range(HALVES):
         received(3, h, agg_in)
         sides = agg_in[:, :, cols[h]].reshape(2 * rows, half)
-        for i in range(CHUNKS):
-            span = pl.ds(i * step, step)
+
+        def deltas(i, carry):
+            span = pl.ds(pl.multiple_of(i * step, step), step)
             grad = own_grad[span, cols[h]] + dot(wide_side_t[span], sides)
             enc_delta[span, cols[h]] = (grad * encoded[span, cols[h]]).astype(BF16)
-
-    def grid_part(i):
-        span = pl.ds(i * step, step)
+            return carry
+
+        lax.fori_loop(0, CHUNKS, deltas, 0)
+
+    def grid_copy(i):
+        span = pl.ds(pl.multiple_of(i * step, step), step)
+        return pltpu.make_async_copy(grid_out.at[span], grid_h.at[0, span], out_sem.at[i])
+
+    def grid_part(i, carry):
+        span = pl.ds(pl.multiple_of(i * step, step), step)
         grid_out[span] = dot_t(enc_delta[span], enc_w[...]).astype(BF16)
-        return local(grid_out.at[span], grid_h.at[0, span], out_sem.at[i])
+        grid_copy(i).start()
+        return carry
 
     if not fused:
         for i in range(CHUNKS):
             part[i] = dot(x_t[i], enc_delta[...]) * scale
         final_copy = local(part, final_h, out_sem.at[CHUNKS + 1])
-        grid_copies = [grid_part(i) for i in range(CHUNKS)]
+        lax.fori_loop(0, CHUNKS, grid_part, 0)
     else:
         share = part.shape[2]
         mine = share // members
@@ -301,13 +320,17 @@
                 device_id={"ens": peer}, device_id_type=MESH)
 
         order = [lax.rem(level + d, levels) for d in list(range(1, levels)) + [0]]
-        for z in order:
+
+        def weigh(n, carry):
+            z = lax.rem(level + 1 + n, levels)
             value = (dot(x_t[z], enc_delta[...]) * scale).reshape(2, share, width)
             part[z] = value
             part_out[z] = value.astype(BF16)
             pair(z).start()
-        grid_copies = [grid_part(0)]
-        for z in order:
+            return carry
+
+        def pair_up(n, carry):
+            z = lax.rem(level + 1 + n, levels)
             pair(z).wait_recv()
             value = part[z, core] + pair_in[z].astype(F32)
             value = value.reshape(members, mine, width)
@@ -315,17 +338,26 @@
             quarter_out[z] = value.astype(BF16)
             for d in range(1, members):
                 across(z, d, False).start()
-        grid_copies += [grid_part(i) for i in range(1, CHUNKS)]
-        for n, z in enumerate(order):
+            return carry
+
+        def add_up(z):
             value = quarter[z, ens]
             for d in range(1, members):
                 across(z, d, True).wait_recv()
                 value = value + ens_in[z, lax.rem(ens + d, members)].astype(F32)
-            if n < levels - 1:
-                summed_out[z] = value.astype(BF16)
-                along(n + 1, False).start()
-            else:
-                summed[...] = value
+            return value
+
+        def pass_on(n, carry):
+            z = lax.rem(level + n, levels)
+            summed_out[z] = add_up(z).astype(BF16)
+            along(n, False).start()
+            return carry
+
+        lax.fori_loop(0, levels, weigh, 0)
+        lax.fori_loop(0, levels, pair_up, 0)
+        lax.fori_loop(0, CHUNKS, grid_part, 0)
+        lax.fori_loop(1, levels, pass_on, 0)
+        summed[...] = add_up(level)
         value = summed[...]
         for d in range(1, levels):
             along(d, True).wait_recv()
@@ -350,8 +382,8 @@
         for h in range(HALVES):
             sent(turn, h, landing)
     result_copy.wait()
-    for copy in grid_copies:
-        copy.wait()
+    for i in range(CHUNKS):
+        grid_copy(i).wait()
     final_copy.wait()
 
 

time: 39 us -> 41.2 us (1.056)
  Pallas kernels: 38.2 us -> 40.4 us
    pallas_call x1, Pallas kernels: 36 us -> 38.2 us  [on_device(): pl.pallas_call(functools.partial(kernel, bands, members, scale, fused), o...]
where the time goes in v4:
time: 41.2 us; the launch traced here: 41 us
  Pallas kernels  40.4 us (98%)
  between operations  0.64 us (2%)
    pallas_call x1, Pallas kernels, on_device(): pl.pallas_call(functools.partial(kernel, bands, members, scale, fused), o...  38.2 us
    pallas_call x1, Pallas kernels, on_device(): pl.pallas_call(leave, out_shape=tuple((jax.ShapeDtypeStruct(a.shape, a.dt...  2.15 us

profile of v4, /device:TPU:0, one launch (start us, length us, event | category | flops | bytes accessed | tf_op | source)
XLA Modules:
  0.0 41.0 jit_solution(17626544011351391673)
XLA Ops:
  0.6 38.2 %shard_map.121 = (bf16[1,128,512]{2,1,0:T(8,128)(2,1)}, bf16[1,1024,512]{2,1,0:T(8,128)(2,1)}, f32[4,16,512]{2,1,0:T(8,128)}) custom-call(bf16[1,1024,512]{2,1,0:T(8,128)(2,1)} %x_h.1, bf16[1,128,512]{2,1,0:T(8,128)(2,1)} %mesh_h.1, bf16[1,128,512]{2,1,0:T(8,128)(2,1)} %cot_h.1, bf16[8,2,128,128]{3,2,1,0:T(8,128)(2,1)} %edge_h.1, s32[2,8]{1,0:T(2,128)} %bitcast.2, ...), custom_call_target="tpu_custom_call" | custom-call | tf_op jit(solution)/shard_map/pallas_call | solution.py:448
  38.8 2.1 %shard_map.122 = (bf16[1,128,512]{2,1,0:T(8,128)(2,1)}, bf16[1,1024,512]{2,1,0:T(8,128)(2,1)}, f32[4,16,512]{2,1,0:T(8,128)}) custom-call(bf16[1,128,512]{2,1,0:T(8,128)(2,1)} %get-tuple-element.9.result, bf16[1,1024,512]{2,1,0:T(8,128)(2,1)} %get-tuple-element.10.grid_grad, f32[4,16,512]{2,1,0:T(8,128)} %get-tuple-element.11.grad), custom_call_target="tpu_custom_call" | custom-call | tf_op jit(solution)/shard_map/pallas_call | solution.py:466

commit v5 on v3

--- a/solution.py
+++ b/solution.py
@@ -18,11 +18,6 @@
     return 0.5 + 0.5 * jnp.tanh(0.5 * value)
 
 
-def slope_of(value):
-    sig = sigmoid(value)
-    return sig * (1.0 + value * (1.0 - sig))
-
-
 def dot(a, b):
     return jnp.dot(a, b, preferred_element_type=F32)
 
@@ -37,7 +32,7 @@
     result_h, grid_h, final_h,
     x, mesh, cot, edge, targets, mweight, sources, enc_w, agg_w, proc_w,
     wide, wide_own_t, wide_side_t, near, near_t, x_t,
-    encoded, panels, panel_out, panel_in, upd, upd_in, push_out, push_in, agg, agg_in,
+    slopes, panels, panel_out, panel_in, upd, upd_in, push_out, push_in, agg, agg_in,
     mesh_slope, mesh_grad, own_grad, enc_delta, grid_out, result,
     part, part_out, pair_in, quarter, quarter_out, ens_in, summed, summed_out, z_in, final, final_out,
     in_sem, out_sem, halo_send, halo_recv, a_send, a_recv, b_send, b_recv, c_send, c_recv, d_send, d_recv,
@@ -136,9 +131,10 @@
                 x_copies[i].wait()
             span = pl.ds(i * step, step)
             value = dot(x[span], enc_w[:, cols[h]])
-            encoded[span, cols[h]] = value
-            message = (value * sigmoid(value)).astype(BF16)
-            term = dot(wide[:, i * step:(i + 1) * step], message)
+            sig = sigmoid(value)
+            message = value * sig
+            slopes[span, cols[h]] = sig + message * (1.0 - sig)
+            term = dot(wide[:, i * step:(i + 1) * step], message.astype(BF16))
             panels[:, cols[h]] = term if i == 0 else panels[:, cols[h]] + term
         if h == 0:
             pl.semaphore_wait(barrier, expected)
@@ -146,12 +142,18 @@
             panel_out[(1 - off) // 2, :, cols[h]] = panels[pl.ds((1 + off) * rows, rows), cols[h]].astype(BF16)
         both(lambda off: halo(0, h, panel_out.at[(1 - off) // 2], panel_in, off).start())
 
-    def slopes(i, carry):
-        span = pl.ds(pl.multiple_of(i * 64, 64), 64)
-        encoded[span] = slope_of(encoded[span])
-        return carry
-
-    lax.fori_loop(0, total // 64, slopes, 0)
+    def turn_edges(target, first, j):
+        for b in range(blocks):
+            span = slice(b * rows, (b + 1) * rows)
+            target[span, first:first + rows] = wide[j * rows:(j + 1) * rows, span].T
+
+    deep = width // CHUNKS
+
+    def turn_x(i):
+        for b in range(blocks):
+            span = slice(b * rows, (b + 1) * rows)
+            x_t[i, :, span] = x[span, i * deep:(i + 1) * deep].T
+
     sources_copy.wait()
     mweight_copy.wait()
     first = mweight[0].astype(F32)
@@ -161,6 +163,8 @@
         mixed = (first * hit[0] + second * hit[1]).astype(BF16)
         near[j] = mixed
         near_t[j] = mixed.T
+    turn_edges(wide_own_t, 0, 1)
+    turn_x(0)
     mesh_copy.wait()
     agg_copy.wait()
 
@@ -182,25 +186,8 @@
 
     own = dot(near[1], upd[...])
 
-    def turn_edges(b, carry):
-        span = pl.ds(pl.multiple_of(b * rows, rows), rows)
-        wide_own_t[span] = wide[rows:2 * rows, span].T
-        wide_side_t[span, 0:rows] = wide[0:rows, span].T
-        wide_side_t[span, rows:2 * rows] = wide[2 * rows:3 * rows, span].T
-        return carry
-
-    deep = width // CHUNKS
-
-    def turn_x(i):
-        def body(b, carry):
-            span = pl.ds(pl.multiple_of(b * rows, rows), rows)
-            x_t[i, :, span] = x[span, i * deep:(i + 1) * deep].T
-            return carry
-
-        lax.fori_loop(0, blocks, body, 0)
-
-    lax.fori_loop(0, blocks, turn_edges, 0)
-    turn_x(0)
+    turn_edges(wide_side_t, 0, 0)
+    turn_edges(wide_side_t, rows, 2)
     proc_copy.wait()
     cot_copy.wait()
 
@@ -240,12 +227,9 @@
                 agg[:, cols[n]] = partial[n].astype(BF16)
                 both(lambda off: halo(3, n, agg, agg_in, off).start())
 
-    def own_part(i, carry):
-        span = pl.ds(pl.multiple_of(i * step, step), step)
+    for i in range(CHUNKS):
+        span = pl.ds(i * step, step)
         own_grad[span] = dot(wide_own_t[span], agg[...])
-        return carry
-
-    lax.fori_loop(0, CHUNKS, own_part, 0)
     turn_x(3)
 
     for h in range(HALVES):
@@ -254,7 +238,7 @@
         for i in range(CHUNKS):
             span = pl.ds(i * step, step)
             grad = own_grad[span, cols[h]] + dot(wide_side_t[span], sides)
-            enc_delta[span, cols[h]] = (grad * encoded[span, cols[h]]).astype(BF16)
+            enc_delta[span, cols[h]] = (grad * slopes[span, cols[h]]).astype(BF16)
 
     def grid_part(i):
         span = pl.ds(i * step, step)
@@ -301,13 +285,13 @@
                 device_id={"ens": peer}, device_id_type=MESH)
 
         order = [lax.rem(level + d, levels) for d in list(range(1, levels)) + [0]]
-        for z in order:
+        def weigh(z):
             value = (dot(x_t[z], enc_delta[...]) * scale).reshape(2, share, width)
             part[z] = value
             part_out[z] = value.astype(BF16)
             pair(z).start()
-        grid_copies = [grid_part(0)]
-        for z in order:
+
+        def pair_up(z):
             pair(z).wait_recv()
             value = part[z, core] + pair_in[z].astype(F32)
             value = value.reshape(members, mine, width)
@@ -315,17 +299,27 @@
             quarter_out[z] = value.astype(BF16)
             for d in range(1, members):
                 across(z, d, False).start()
-        grid_copies += [grid_part(i) for i in range(1, CHUNKS)]
-        for n, z in enumerate(order):
+
+        def add_up(z):
             value = quarter[z, ens]
             for d in range(1, members):
                 across(z, d, True).wait_recv()
                 value = value + ens_in[z, lax.rem(ens + d, members)].astype(F32)
-            if n < levels - 1:
-                summed_out[z] = value.astype(BF16)
-                along(n + 1, False).start()
-            else:
-                summed[...] = value
+            return value
+
+        weigh(order[0])
+        for n in range(1, levels):
+            weigh(order[n])
+            pair_up(order[n - 1])
+        grid_copies = [grid_part(0)]
+        pair_up(order[-1])
+        grid_copies.append(grid_part(1))
+        for n in range(levels - 1):
+            summed_out[order[n]] = add_up(order[n]).astype(BF16)
+            along(n + 1, False).start()
+            if n + 2 < CHUNKS:
+                grid_copies.append(grid_part(n + 2))
+        summed[...] = add_up(level)
         value = summed[...]
         for d in range(1, levels):
             along(d, True).wait_recv()

time: 39 us -> 38.5 us (0.987)
  Pallas kernels: 38.2 us -> 37.7 us
    pallas_call x1, Pallas kernels: 36 us -> 35.6 us  [on_device(): pl.pallas_call(functools.partial(kernel, bands, members, scale, fused), o...]
where the time goes in v5:
time: 38.5 us; the launch traced here: 38.4 us
  Pallas kernels  37.7 us (98%)
  between operations  0.64 us (2%)
    pallas_call x1, Pallas kernels, on_device(): pl.pallas_call(functools.partial(kernel, bands, members, scale, fused), o...  35.6 us
    pallas_call x1, Pallas kernels, on_device(): pl.pallas_call(leave, out_shape=tuple((jax.ShapeDtypeStruct(a.shape, a.dt...  2.15 us

profile of v5, /device:TPU:0, one launch (start us, length us, event | category | flops | bytes accessed | tf_op | source)
XLA Modules:
  0.0 38.4 jit_solution(11910115080611502248)
XLA Ops:
  0.6 35.6 %shard_map.121 = (bf16[1,128,512]{2,1,0:T(8,128)(2,1)}, bf16[1,1024,512]{2,1,0:T(8,128)(2,1)}, f32[4,16,512]{2,1,0:T(8,128)}) custom-call(bf16[1,1024,512]{2,1,0:T(8,128)(2,1)} %x_h.1, bf16[1,128,512]{2,1,0:T(8,128)(2,1)} %mesh_h.1, bf16[1,128,512]{2,1,0:T(8,128)(2,1)} %cot_h.1, bf16[8,2,128,128]{3,2,1,0:T(8,128)(2,1)} %edge_h.1, s32[2,8]{1,0:T(2,128)} %bitcast.2, ...), custom_call_target="tpu_custom_call" | custom-call | tf_op jit(solution)/shard_map/pallas_call | solution.py:410
  36.2 2.1 %shard_map.122 = (bf16[1,128,512]{2,1,0:T(8,128)(2,1)}, bf16[1,1024,512]{2,1,0:T(8,128)(2,1)}, f32[4,16,512]{2,1,0:T(8,128)}) custom-call(bf16[1,128,512]{2,1,0:T(8,128)(2,1)} %get-tuple-element.9.result, bf16[1,1024,512]{2,1,0:T(8,128)(2,1)} %get-tuple-element.10.grid_grad, f32[4,16,512]{2,1,0:T(8,128)} %get-tuple-element.11.grad), custom_call_target="tpu_custom_call" | custom-call | tf_op jit(solution)/shard_map/pallas_call | solution.py:428

commit v6 on v5

--- a/solution.py
+++ b/solution.py
@@ -152,7 +152,7 @@
     def turn_x(i):
         for b in range(blocks):
             span = slice(b * rows, (b + 1) * rows)
-            x_t[i, :, span] = x[span, i * deep:(i + 1) * deep].T
+            x_t[i * deep:(i + 1) * deep, span] = x[span, i * deep:(i + 1) * deep].T
 
     sources_copy.wait()
     mweight_copy.wait()
@@ -232,7 +232,7 @@
         own_grad[span] = dot(wide_own_t[span], agg[...])
     turn_x(3)
 
-    for h in range(HALVES):
+    def deltas(h):
         received(3, h, agg_in)
         sides = agg_in[:, :, cols[h]].reshape(2 * rows, half)
         for i in range(CHUNKS):
@@ -246,99 +246,107 @@
         return local(grid_out.at[span], grid_h.at[0, span], out_sem.at[i])
 
     if not fused:
-        for i in range(CHUNKS):
-            part[i] = dot(x_t[i], enc_delta[...]) * scale
+        for h in range(HALVES):
+            deltas(h)
+            part[:, cols[h]] = dot(x_t[...], enc_delta[:, cols[h]]) * scale
         final_copy = local(part, final_h, out_sem.at[CHUNKS + 1])
         grid_copies = [grid_part(i) for i in range(CHUNKS)]
     else:
-        share = part.shape[2]
+        share = part.shape[3]
         mine = share // members
 
-        def pair(z):
+        def pair(h):
             return pltpu.make_async_remote_copy(
-                src_ref=part_out.at[z, 1 - core], dst_ref=pair_in.at[z],
-                send_sem=a_send.at[z], recv_sem=a_recv.at[z],
+                src_ref=part_out.at[h, 1 - core], dst_ref=pair_in.at[h],
+                send_sem=a_send.at[h], recv_sem=a_recv.at[h],
                 device_id={"grid": me + 1 - 2 * core}, device_id_type=MESH)
 
-        def across(z, d, arriving):
+        def across(h, d, arriving):
             peer = lax.rem(ens + d, members)
             slot = peer if arriving else ens
             return pltpu.make_async_remote_copy(
-                src_ref=quarter_out.at[z, peer], dst_ref=ens_in.at[z, slot],
-                send_sem=b_send.at[z, peer], recv_sem=b_recv.at[z, slot],
+                src_ref=quarter_out.at[h, peer], dst_ref=ens_in.at[h, slot],
+                send_sem=b_send.at[h, peer], recv_sem=b_recv.at[h, slot],
                 device_id={"ens": peer}, device_id_type=MESH)
 
-        def along(d, arriving):
+        def along(h, d, arriving):
             peer = lax.rem(level + d, levels)
             slot = peer if arriving else level
             return pltpu.make_async_remote_copy(
-                src_ref=summed_out.at[peer], dst_ref=z_in.at[slot],
-                send_sem=c_send.at[peer], recv_sem=c_recv.at[slot],
+                src_ref=summed_out.at[h, peer], dst_ref=z_in.at[h, slot],
+                send_sem=c_send.at[h, peer], recv_sem=c_recv.at[h, slot],
                 device_id={"grid": peer * 2 + core}, device_id_type=MESH)
 
-        def gather(d, arriving):
+        def gather(h, d, arriving):
             peer = lax.rem(ens + d, members)
             slot = peer if arriving else ens
             return pltpu.make_async_remote_copy(
-                src_ref=final.at[ens], dst_ref=final.at[slot],
-                send_sem=d_send.at[peer], recv_sem=d_recv.at[slot],
+                src_ref=final.at[h, ens], dst_ref=final.at[h, slot],
+                send_sem=d_send.at[h, peer], recv_sem=d_recv.at[h, slot],
                 device_id={"ens": peer}, device_id_type=MESH)
 
-        order = [lax.rem(level + d, levels) for d in list(range(1, levels)) + [0]]
-        def weigh(z):
-            value = (dot(x_t[z], enc_delta[...]) * scale).reshape(2, share, width)
-            part[z] = value
-            part_out[z] = value.astype(BF16)
-            pair(z).start()
-
-        def pair_up(z):
-            pair(z).wait_recv()
-            value = part[z, core] + pair_in[z].astype(F32)
-            value = value.reshape(members, mine, width)
-            quarter[z] = value
-            quarter_out[z] = value.astype(BF16)
+        def weigh(h):
+            value = (dot(x_t[...], enc_delta[:, cols[h]]) * scale).reshape(levels, 2, share, half)
+            for c in range(2):
+                part[h, c] = value[:, c]
+                part_out[h, c] = value[:, c].astype(BF16)
+            pair(h).start()
+
+        def pair_up(h):
+            pair(h).wait_recv()
+            value = part[h, core] + pair_in[h].astype(F32)
+            for q in range(members):
+                block = value[:, q * mine:(q + 1) * mine]
+                quarter[h, q] = block
+                quarter_out[h, q] = block.astype(BF16)
             for d in range(1, members):
-                across(z, d, False).start()
-
-        def add_up(z):
-            value = quarter[z, ens]
+                across(h, d, False).start()
+
+        def add_up(h):
+            value = quarter[h, ens]
             for d in range(1, members):
-                across(z, d, True).wait_recv()
-                value = value + ens_in[z, lax.rem(ens + d, members)].astype(F32)
-            return value
-
-        weigh(order[0])
-        for n in range(1, levels):
-            weigh(order[n])
-            pair_up(order[n - 1])
+                across(h, d, True).wait_recv()
+                value = value + ens_in[h, lax.rem(ens + d, members)].astype(F32)
+            summed[h] = value
+            summed_out[h] = value.astype(BF16)
+            for d in range(1, levels):
+                along(h, d, False).start()
+
+        def finish(h):
+            value = summed[h, level]
+            for d in range(1, levels):
+                along(h, d, True).wait_recv()
+                value = value + z_in[h, lax.rem(level + d, levels)].astype(F32)
+            final[h, ens] = value.astype(BF16)
+            for d in range(1, members):
+                gather(h, d, False).start()
+
+        deltas(0)
+        weigh(0)
+        deltas(1)
+        pair_up(0)
+        weigh(1)
         grid_copies = [grid_part(0)]
-        pair_up(order[-1])
-        grid_copies.append(grid_part(1))
-        for n in range(levels - 1):
-            summed_out[order[n]] = add_up(order[n]).astype(BF16)
-            along(n + 1, False).start()
-            if n + 2 < CHUNKS:
-                grid_copies.append(grid_part(n + 2))
-        summed[...] = add_up(level)
-        value = summed[...]
-        for d in range(1, levels):
-            along(d, True).wait_recv()
-            value = value + z_in[lax.rem(level + d, levels)].astype(F32)
-        final[ens] = value.astype(BF16)
-        for d in range(1, members):
-            gather(d, False).start()
-        for d in range(1, members):
-            gather(d, True).wait_recv()
-        final_out[...] = final[...].astype(F32)
+        pair_up(1)
+        grid_copies += [grid_part(1), grid_part(2)]
+        add_up(0)
+        grid_copies.append(grid_part(3))
+        add_up(1)
+        for h in range(HALVES):
+            finish(h)
+        for h in range(HALVES):
+            for d in range(1, members):
+                gather(h, d, True).wait_recv()
+        for h in range(HALVES):
+            final_out[:, :, cols[h]] = final[h].astype(F32)
         final_copy = local(final_out, final_h, out_sem.at[CHUNKS + 1])
-        for z in order:
-            pair(z).wait_send()
+        for h in range(HALVES):
+            pair(h).wait_send()
             for d in range(1, members):
-                across(z, d, False).wait_send()
-        for d in range(1, levels):
-            along(d, False).wait_send()
-        for d in range(1, members):
-            gather(d, False).wait_send()
+                across(h, d, False).wait_send()
+                gather(h, d, False).wait_send()
+            for d in range(1, levels):
+                along(h, d, False).wait_send()
 
     for turn, landing in enumerate((panel_in, upd_in, push_in, agg_in)):
         for h in range(HALVES):
@@ -378,12 +386,14 @@
     fused = bands % 2 == 0 and levels == CHUNKS and share % (16 * members) == 0
     scale = 1.0 / float(members * total * bands) ** 0.5
     mine = share // members if fused else 16
-    gshape = (CHUNKS, 2, width // CHUNKS // 2, width) if fused else (CHUNKS, width // CHUNKS, width)
+    half = width // HALVES
+    gshape = (HALVES, 2, CHUNKS, width // CHUNKS // 2, half) if fused else (width, width)
     last = (members, mine, width) if fused else gshape
     vm = pltpu.VMEM
     dma = pltpu.SemaphoreType.DMA
     panel = (2, rows, width)
-    quarters = (CHUNKS, members, mine, width)
+    quarters = (HALVES, members, CHUNKS, mine, half)
+    levelled = (HALVES, CHUNKS, mine, half)
     scratch = [
         vm((total, width), BF16), vm((rows, width), BF16), vm((rows, width), BF16),
         vm(edge_weights.shape, BF16),
@@ -391,19 +401,19 @@
         pltpu.SMEM(mesh_sources.shape, jnp.int32),
         vm((width, width), BF16), vm((width, width), BF16), vm((width, width), BF16),
         vm((3 * rows, total), BF16), vm((total, rows), BF16), vm((total, 2 * rows), BF16),
-        vm((3, rows, rows), BF16), vm((3, rows, rows), BF16), vm((CHUNKS, width // CHUNKS, total), BF16),
+        vm((3, rows, rows), BF16), vm((3, rows, rows), BF16), vm((width, total), BF16),
         vm((total, width), F32), vm((3 * rows, width), F32),
         vm(panel, BF16), vm(panel, BF16), vm((rows, width), BF16), vm(panel, BF16),
         vm(panel, BF16), vm(panel, BF16), vm((rows, width), BF16), vm(panel, BF16),
         vm((rows, width), F32), vm((rows, width), F32),
         vm((total, width), F32), vm((total, width), BF16), vm((total, width), BF16), vm((rows, width), BF16),
-        vm(gshape, F32), vm(gshape, BF16), vm((CHUNKS, width // CHUNKS // 2, width), BF16),
+        vm(gshape, F32), vm(gshape, BF16), vm((HALVES, CHUNKS, width // CHUNKS // 2, half), BF16),
         vm(quarters, F32), vm(quarters, BF16), vm(quarters, BF16),
-        vm((mine, width), F32), vm((CHUNKS, mine, width), BF16), vm((CHUNKS, mine, width), BF16),
-        vm((members, mine, width), BF16), vm((members, mine, width), F32),
+        vm(levelled, F32), vm(levelled, BF16), vm(levelled, BF16),
+        vm((HALVES, members, mine, half), BF16), vm((members, mine, width), F32),
         dma((9 + CHUNKS,)), dma((CHUNKS + 2,)), dma((4, 2, HALVES)), dma((4, 2, HALVES)),
-        dma((CHUNKS,)), dma((CHUNKS,)), dma((CHUNKS, members)), dma((CHUNKS, members)),
-        dma((CHUNKS,)), dma((CHUNKS,)), dma((members,)), dma((members,)),
+        dma((HALVES,)), dma((HALVES,)), dma((HALVES, members)), dma((HALVES, members)),
+        dma((HALVES, CHUNKS)), dma((HALVES, CHUNKS)), dma((HALVES, members)), dma((HALVES, members)),
     ]
     hbm = pl.BlockSpec(memory_space=pltpu.HBM)
     anywhere = pl.BlockSpec(memory_space=pl.ANY)

time: 38.5 us -> 40.1 us (1.042)
  Pallas kernels: 37.7 us -> 39.3 us
    pallas_call x1, Pallas kernels: 35.6 us -> 37.1 us  [on_device(): pl.pallas_call(functools.partial(kernel, bands, members, scale, fused), o...]
where the time goes in v6:
time: 40.1 us; the launch traced here: 39.9 us
  Pallas kernels  39.3 us (98%)
  between operations  0.64 us (2%)
    pallas_call x1, Pallas kernels, on_device(): pl.pallas_call(functools.partial(kernel, bands, members, scale, fused), o...  37.1 us
    pallas_call x1, Pallas kernels, on_device(): pl.pallas_call(leave, out_shape=tuple((jax.ShapeDtypeStruct(a.shape, a.dt...  2.15 us

profile of v6, /device:TPU:0, one launch (start us, length us, event | category | flops | bytes accessed | tf_op | source)
XLA Modules:
  0.0 39.9 jit_solution(15254177842889506673)
XLA Ops:
  0.6 37.1 %shard_map.121 = (bf16[1,128,512]{2,1,0:T(8,128)(2,1)}, bf16[1,1024,512]{2,1,0:T(8,128)(2,1)}, f32[4,16,512]{2,1,0:T(8,128)}) custom-call(bf16[1,1024,512]{2,1,0:T(8,128)(2,1)} %x_h.1, bf16[1,128,512]{2,1,0:T(8,128)(2,1)} %mesh_h.1, bf16[1,128,512]{2,1,0:T(8,128)(2,1)} %cot_h.1, bf16[8,2,128,128]{3,2,1,0:T(8,128)(2,1)} %edge_h.1, s32[2,8]{1,0:T(2,128)} %bitcast.2, ...), custom_call_target="tpu_custom_call" | custom-call | tf_op jit(solution)/shard_map/pallas_call | solution.py:420
  37.8 2.1 %shard_map.122 = (bf16[1,128,512]{2,1,0:T(8,128)(2,1)}, bf16[1,1024,512]{2,1,0:T(8,128)(2,1)}, f32[4,16,512]{2,1,0:T(8,128)}) custom-call(bf16[1,128,512]{2,1,0:T(8,128)(2,1)} %get-tuple-element.9.result, bf16[1,1024,512]{2,1,0:T(8,128)(2,1)} %get-tuple-element.10.grid_grad, f32[4,16,512]{2,1,0:T(8,128)} %get-tuple-element.11.grad), custom_call_target="tpu_custom_call" | custom-call | tf_op jit(solution)/shard_map/pallas_call | solution.py:438

commit v7 on v5

--- a/solution.py
+++ b/solution.py
@@ -232,7 +232,7 @@
         own_grad[span] = dot(wide_own_t[span], agg[...])
     turn_x(3)
 
-    for h in range(HALVES):
+    def deltas(h):
         received(3, h, agg_in)
         sides = agg_in[:, :, cols[h]].reshape(2 * rows, half)
         for i in range(CHUNKS):
@@ -246,6 +246,8 @@
         return local(grid_out.at[span], grid_h.at[0, span], out_sem.at[i])
 
     if not fused:
+        for h in range(HALVES):
+            deltas(h)
         for i in range(CHUNKS):
             part[i] = dot(x_t[i], enc_delta[...]) * scale
         final_copy = local(part, final_h, out_sem.at[CHUNKS + 1])
@@ -260,6 +262,9 @@
                 send_sem=a_send.at[z], recv_sem=a_recv.at[z],
                 device_id={"grid": me + 1 - 2 * core}, device_id_type=MESH)
 
+        odd = lax.rem(ens, 2)
+        first_far = (3 - 2 * odd, 2, 1 + 2 * odd) if members == 4 else tuple(range(1, members))
+
         def across(z, d, arriving):
             peer = lax.rem(ens + d, members)
             slot = peer if arriving else ens
@@ -285,11 +290,12 @@
                 device_id={"ens": peer}, device_id_type=MESH)
 
         order = [lax.rem(level + d, levels) for d in list(range(1, levels)) + [0]]
-        def weigh(z):
-            value = (dot(x_t[z], enc_delta[...]) * scale).reshape(2, share, width)
-            part[z] = value
-            part_out[z] = value.astype(BF16)
-            pair(z).start()
+        def weigh(z, h):
+            value = (dot(x_t[z], enc_delta[:, cols[h]]) * scale).reshape(2, share, half)
+            part[z, :, :, cols[h]] = value
+            part_out[z, :, :, cols[h]] = value.astype(BF16)
+            if h == HALVES - 1:
+                pair(z).start()
 
         def pair_up(z):
             pair(z).wait_recv()
@@ -297,7 +303,7 @@
             value = value.reshape(members, mine, width)
             quarter[z] = value
             quarter_out[z] = value.astype(BF16)
-            for d in range(1, members):
+            for d in first_far:
                 across(z, d, False).start()
 
         def add_up(z):
@@ -307,9 +313,14 @@
                 value = value + ens_in[z, lax.rem(ens + d, members)].astype(F32)
             return value
 
-        weigh(order[0])
+        for h in range(HALVES - 1):
+            deltas(h)
+            for z in order:
+                weigh(z, h)
+        deltas(HALVES - 1)
+        weigh(order[0], HALVES - 1)
         for n in range(1, levels):
-            weigh(order[n])
+            weigh(order[n], HALVES - 1)
             pair_up(order[n - 1])
         grid_copies = [grid_part(0)]
         pair_up(order[-1])

time: 38.5 us -> 38.7 us (level)
  no operation moved by 1% of the time
where the time goes in v7:
time: 38.7 us; the launch traced here: 38.5 us
  Pallas kernels  37.9 us (98%)
  between operations  0.64 us (2%)
    pallas_call x1, Pallas kernels, on_device(): pl.pallas_call(functools.partial(kernel, bands, members, scale, fused), o...  35.7 us
    pallas_call x1, Pallas kernels, on_device(): pl.pallas_call(leave, out_shape=tuple((jax.ShapeDtypeStruct(a.shape, a.dt...  2.15 us

profile of v7, /device:TPU:0, one launch (start us, length us, event | category | flops | bytes accessed | tf_op | source)
XLA Modules:
  0.0 38.5 jit_solution(12964267569774420450)
XLA Ops:
  0.6 35.7 %shard_map.121 = (bf16[1,128,512]{2,1,0:T(8,128)(2,1)}, bf16[1,1024,512]{2,1,0:T(8,128)(2,1)}, f32[4,16,512]{2,1,0:T(8,128)}) custom-call(bf16[1,1024,512]{2,1,0:T(8,128)(2,1)} %x_h.1, bf16[1,128,512]{2,1,0:T(8,128)(2,1)} %mesh_h.1, bf16[1,128,512]{2,1,0:T(8,128)(2,1)} %cot_h.1, bf16[8,2,128,128]{3,2,1,0:T(8,128)(2,1)} %edge_h.1, s32[2,8]{1,0:T(2,128)} %bitcast.2, ...), custom_call_target="tpu_custom_call" | custom-call | tf_op jit(solution)/shard_map/pallas_call | solution.py:421
  36.3 2.1 %shard_map.122 = (bf16[1,128,512]{2,1,0:T(8,128)(2,1)}, bf16[1,1024,512]{2,1,0:T(8,128)(2,1)}, f32[4,16,512]{2,1,0:T(8,128)}) custom-call(bf16[1,128,512]{2,1,0:T(8,128)(2,1)} %get-tuple-element.9.result, bf16[1,1024,512]{2,1,0:T(8,128)(2,1)} %get-tuple-element.10.grid_grad, f32[4,16,512]{2,1,0:T(8,128)} %get-tuple-element.11.grad), custom_call_target="tpu_custom_call" | custom-call | tf_op jit(solution)/shard_map/pallas_call | solution.py:439
